TPU v7x, 512 devices: a whole 4x8x8 slice. The times are simulated.
512 devices in a mesh: gx: 32 (over x_hi, z, core), gy: 16 (over y, x_lo).
Axes of the slice: x: 4 (x_hi: 2, x_lo: 2; x = x_hi * 2 + x_lo), y: 8, z: 8, core: 2. Of those that a mesh axis runs over, the one named last changes fastest.
Arguments:
- voltages: bfloat16 [2, 2048, 1024, 128], P(None, 'gx', 'gy'), may hold values from -6 to 6
- beam_grid: int32 [1024, 2], replicated, may hold values from 0 to 255
- feed_pos: int32 [2048, 2], replicated, may hold values from 0 to 255
- rfi_mask: int32 [8, 16384], P(None, ('gy', 'gx')), may hold values 0 or 1
Outputs:
- power: bfloat16 [1024, 8, 16384], P(('gx', 'gy'))
- sk_sums: float32 [2, 1024, 16384], P(None, ('gx', 'gy'))
All inputs are finite; a program needn't handle non-finite values. No bound on the sum of `rfi_mask` on one device may be relied on, other than what follows from the above.
Results may differ from a plain program's by a relative error of at most 0.0056.
Values may be sent and summed in bfloat16 or wider, within the bound.
No kernel may reach another device: no remote copies, remote signals or barrier semaphores. Data moves between devices by JAX's collectives and lax.ppermute only.
A program may use at most 64 MiB of HBM per device.

v0:
```python
import math

import jax
import jax.numpy as jnp
from jax import lax
from jax.sharding import PartitionSpec as P

FEEDS = 2048
BEAMS = 1024
UPCHAN = 16
TOUT = 8
TIME = 128


def dft_tables(time_len, upchan):
    rows = jnp.arange(time_len, dtype=jnp.int32)[:, None]
    cols = jnp.arange(time_len, dtype=jnp.int32)[None, :]
    same = (rows // upchan == cols // upchan).astype(jnp.float32)
    turns = rows % upchan * (cols % upchan) % upchan
    angle = turns.astype(jnp.float32) * (2.0 * math.pi / upchan)
    scale = 1.0 / math.sqrt(upchan)
    return (jnp.cos(angle) * same * scale, jnp.sin(angle) * same * scale)


def steering(grid_base, chan, feeds):
    turns = grid_base * ((chan + 400) % 4096) % 4096
    angle = turns.astype(jnp.float32) * (2.0 * math.pi / 4096.0)
    scale = 1.0 / math.sqrt(feeds)
    return jnp.concatenate([jnp.cos(angle) * scale, -jnp.sin(angle) * scale], 0).astype(
        jnp.bfloat16
    )


def per_device(voltages, beam_grid, feed_pos, rfi_mask):
    input_count = lax.axis_size("gx")
    chan_count = lax.axis_size("gy")
    chan_dev = voltages.shape[2]
    local_chans = chan_dev // input_count
    first_chan = lax.axis_index("gy") * chan_dev + lax.axis_index("gx") * local_chans
    grid_base = (
        beam_grid[:, 0:1] * feed_pos[None, :, 0] + beam_grid[:, 1:2] * feed_pos[None, :, 1]
    ) % 4096
    weight_stacks = [steering(grid_base, first_chan + which, FEEDS) for which in range(local_chans)]
    piece = lax.all_to_all(voltages, "gx", split_axis=2, concat_axis=1, tiled=True)
    real_list = []
    imag_list = []
    for which in range(local_chans):
        first = jnp.dot(
            weight_stacks[which], piece[0, :, which, :], preferred_element_type=jnp.float32
        )
        second = jnp.dot(
            weight_stacks[which], piece[1, :, which, :], preferred_element_type=jnp.float32
        )
        real_list.append(first[:BEAMS] - second[BEAMS:])
        imag_list.append(second[:BEAMS] + first[BEAMS:])
    real_part = jnp.stack(real_list, 0)
    imag_part = jnp.stack(imag_list, 0)
    cos_table, sin_table = dft_tables(TIME, UPCHAN)
    hig = lax.Precision.HIGHEST
    real_rows = real_part.reshape(local_chans * BEAMS, TIME)
    imag_rows = imag_part.reshape(local_chans * BEAMS, TIME)
    fine_real = jnp.dot(real_rows, cos_table, precision=hig) + jnp.dot(
        imag_rows, sin_table, precision=hig
    )
    fine_imag = jnp.dot(imag_rows, cos_table, precision=hig) - jnp.dot(
        real_rows, sin_table, precision=hig
    )
    intensity = (fine_real * fine_real + fine_imag * fine_imag).reshape(
        local_chans, BEAMS, TOUT, UPCHAN
    )
    bandpass = jnp.mean(intensity, axis=(1, 2)) + 1e-06
    flags = rfi_mask.reshape(TOUT, local_chans, UPCHAN).transpose(1, 0, 2).astype(jnp.float32)
    scaled = intensity / bandpass[:, None, None, :] * flags[:, None, :, :]
    power_local = scaled.astype(jnp.bfloat16).reshape(local_chans, BEAMS, TIME)
    beam_local = BEAMS // (input_count * chan_count)
    gathered = lax.all_to_all(
        lax.all_to_all(power_local, "gx", split_axis=1, concat_axis=0, tiled=True),
        "gy",
        split_axis=1,
        concat_axis=0,
        tiled=True,
    )
    total_chans = gathered.shape[0]
    power = gathered.reshape(total_chans, beam_local, TOUT, UPCHAN).transpose(1, 2, 0, 3)
    power = power.reshape(beam_local, TOUT, total_chans * UPCHAN)
    values = power.astype(jnp.float32)
    sk_sums = jnp.stack([jnp.sum(values, axis=1), jnp.sum(values * values, axis=1)], 0)
    return (power, sk_sums)


def solution(mesh):
    in_specs = (P(None, "gx", "gy", None), P(), P(), P(None, ("gy", "gx")))
    out_specs = (P(("gx", "gy"), None, None), P(None, ("gx", "gy"), None))
    return jax.shard_map(
        per_device, mesh=mesh, in_specs=in_specs, out_specs=out_specs, check_vma=False
    )
```

profile of v0, /device:TPU:1, one launch (start us, length us, event | category | flops | bytes accessed | tf_op | source)
XLA Modules:
  0.0 183.3 jit_solution(16868968671823676465)
XLA Ops:
  0.6 0.0 copy-start.6
  0.6 0.0 copy-start.5
  0.7 0.0 copy-start.4
  0.7 4.3 %copy.31 = bf16[2,64,64,128]{3,1,0,2:T(8,128)(2,1)} copy(bf16[2,64,64,128]{3,2,1,0:T(8,128)(2,1)} %param.4) | data formatting | bytes 4194304 | tf_op args[0]
  5.0 14.4 %all-to-all-start = ((bf16[2,64,64,128]{3,1,0,2:T(8,128)(2,1)}), bf16[2,64,64,128]{3,1,0,2:T(8,128)(2,1)S(1)}, u32[]{:S(2)}, u32[]{:S(2)}) async-start(bf16[2,64,64,128]{3,1,0,2:T(8,128)(2,1)} %copy.31), calls=%async_computation | async-start | bytes 4194304 | tf_op jit(solution)/shard_map/all_to_all | solution.py:44
  19.4 0.0 copy-done.6
  19.4 0.1 convert_element_type.40
  19.5 0.1 mul.187
  19.6 0.0 copy-done.5
  19.6 0.0 copy-done.4
  19.7 74.2 %multiply_convert_fusion.3 = (bf16[1024,2048]{1,0:T(8,128)(2,1)}, bf16[1024,2048]{1,0:T(8,128)(2,1)}, bf16[1024,2048]{1,0:T(8,128)(2,1)}, bf16[1024,2048]{1,0:T(8,128)(2,1)}) fusion(s32[]{:T(128)S(6)} %select_n.88, s32[2048]{0:T(1024)S(1)} %bitcast.71, s32[1024]{0:T(1024)S(1)} %bitcast.74, s32[2048]{0:T(1024)S(1)} %bitcast.70, s32[1024]{0:T(1024)S(1)} %bitcast.73, ...), kind=kLoop, calls=%fused_computation.21 | loop fusion | flops 109051904 | bytes 16801800 | tf_op jit(solution)/shard_map/convert.2
  93.9 0.0 all-to-all-done
  93.9 0.0 copy-start.2
  93.9 0.2 copy.33
  94.1 2.0 %copy-done.2 = bf16[1024,2048]{1,0:T(8,128)(2,1)S(1)} copy-done((bf16[1024,2048]{1,0:T(8,128)(2,1)S(1)}, bf16[1024,2048]{1,0:T(8,128)(2,1)}, u32[]{:S(2)}) %copy-start.2) | copy-done | bytes 4194328
  96.1 4.5 %fusion.9 = f32[2048,128]{1,0:T(8,128)S(1)} fusion(bf16[1024,2048]{1,0:T(8,128)(2,1)} %get-tuple-element.11, bf16[1024,2048]{1,0:T(8,128)(2,1)S(1)} %copy-done.2, bf16[2,2048,2,128]{3,1,2,0:T(8,128)(2,1)S(1)} %bitcast.64), kind=kOutput, calls=%fused_computation.24 | convolution fusion | flops 1090519040 | bytes 9961472 | tf_op jit(solution)/shard_map/dot_general | solution.py:51
  100.7 2.4 %fusion.10 = f32[2048,128]{1,0:T(8,128)S(1)} fusion(bf16[1024,2048]{1,0:T(8,128)(2,1)S(1)} %copy-done.3, bf16[1024,2048]{1,0:T(8,128)(2,1)S(1)} %copy-done.2, bf16[2,2048,2,128]{3,1,2,0:T(8,128)(2,1)S(1)} %bitcast.65), kind=kOutput, calls=%fused_computation.25 | convolution fusion | flops 1090519040 | bytes 9961472 | tf_op jit(solution)/shard_map/dot_general | solution.py:48
  103.1 1.1 copy-done.1
  104.1 2.4 %fusion.7 = f32[2048,128]{1,0:T(8,128)S(1)} fusion(bf16[1024,2048]{1,0:T(8,128)(2,1)S(1)} %copy-done, bf16[1024,2048]{1,0:T(8,128)(2,1)S(1)} %copy-done.1, bf16[2,2048,2,128]{3,1,2,0:T(8,128)(2,1)S(1)} %bitcast.66), kind=kOutput, calls=%fused_computation.22 | convolution fusion | flops 1090519040 | bytes 9961472 | tf_op jit(solution)/shard_map/dot_general | solution.py:51
  106.5 2.4 %fusion.8 = f32[2048,128]{1,0:T(8,128)S(1)} fusion(bf16[1024,2048]{1,0:T(8,128)(2,1)S(1)} %copy-done, bf16[1024,2048]{1,0:T(8,128)(2,1)S(1)} %copy-done.1, bf16[2,2048,2,128]{3,1,2,0:T(8,128)(2,1)S(1)} %bitcast.67), kind=kOutput, calls=%fused_computation.23 | convolution fusion | flops 1090519040 | bytes 9961472 | tf_op jit(solution)/shard_map/dot_general | solution.py:48
  108.9 0.1 fusion.18
  109.0 0.1 fusion.17
  109.1 0.1 pad_maximum_fusion.6
  109.2 1.3 fusion.28
  110.5 1.3 fusion.30
  111.8 1.3 fusion.13
  113.1 1.5 fusion.12
  114.7 0.3 copy.34
  115.0 0.9 reshape.147
  115.9 0.4 reduce_sum.27
  116.3 0.1 copy.35
  116.4 0.1 div.42
  116.5 0.8 fusion.16
  117.3 27.7 %all_to_all.51 = bf16[2,1024,128]{2,0,1:T(2,128)(2,1)S(1)} all-to-all(bf16[2,1024,128]{2,0,1:T(2,128)(2,1)S(1)} %fusion.16), channel_id=1, replica_groups=mesh['gx'=32,'gy'=16] {'gx'}, dimensions={1} | all-to-all | bytes 1048576 | tf_op jit(solution)/shard_map/all_to_all | solution.py:77
  145.0 0.1 copy.38
  145.1 0.1 copy.39
  145.1 0.2 copy.40
  145.3 20.7 %all_to_all.52 = bf16[64,32,128]{2,0,1:T(8,128)(2,1)S(1)} all-to-all(bf16[64,32,128]{2,0,1:T(8,128)(2,1)S(1)} %copy.40), channel_id=1, replica_groups=mesh['gx'=32,'gy'=16] {'gy'}, dimensions={1} | all-to-all | bytes 1048576 | tf_op jit(solution)/shard_map/all_to_all | solution.py:76
  166.0 0.8 copy.41
  166.8 0.7 reshape.148
  167.5 0.1 convert_reduce_fusion
  167.7 0.3 copy.43
  168.0 0.6 stack.33
  168.6 0.3 copy.44
  168.9 0.6 stack.34
  169.5 3.1 %copy.42 = bf16[2,8,1024,16]{3,2,1,0:T(8,128)(2,1)} copy(bf16[2,8,1024,16]{2,3,1,0:T(8,128)(2,1)S(1)} %bitcast.61) | data formatting | bytes 1048576 | tf_op jit(solution)/shard_map/transpose | solution.py:84
  172.6 9.9 %reshape.149 = bf16[2,8,16384]{2,1,0:T(8,128)(2,1)} reshape(bf16[2,8,1024,16]{3,2,1,0:T(8,128)(2,1)} %copy.42) | data formatting | bytes 1048576 | tf_op jit(solution)/shard_map/reshape | solution.py:85
  182.5 0.8 pad_maximum_fusion.8
  (12 shorter events, 0.1 us)
Async XLA Ops:
  0.6 18.8 %copy-start.6 = (s32[8,32]{1,0:T(8,128)S(1)}, s32[8,32]{1,0:T(8,128)}, u32[]{:S(2)}) copy-start(s32[8,32]{1,0:T(8,128)} %param.7) | copy-start | bytes 3076
  0.6 19.0 %copy-start.5 = (s32[1024,2]{0,1:T(2,128)S(1)}, s32[1024,2]{0,1:T(2,128)}, u32[]{:S(2)}) copy-start(s32[1024,2]{0,1:T(2,128)} %param.5) | copy-start | bytes 24580
  0.7 19.0 %copy-start.4 = (s32[2048,2]{0,1:T(2,128)S(1)}, s32[2048,2]{0,1:T(2,128)}, u32[]{:S(2)}) copy-start(s32[2048,2]{0,1:T(2,128)} %param.6) | copy-start | bytes 49156
  5.0 88.9 %all-to-all-start = ((bf16[2,64,64,128]{3,1,0,2:T(8,128)(2,1)}), bf16[2,64,64,128]{3,1,0,2:T(8,128)(2,1)S(1)}, u32[]{:S(2)}, u32[]{:S(2)}) async-start(bf16[2,64,64,128]{3,1,0,2:T(8,128)(2,1)} %copy.31), calls=%async_computation | async-start | bytes 4194304 | tf_op jit(solution)/shard_map/all_to_all | solution.py:44
  93.9 2.2 %copy-start.2 = (bf16[1024,2048]{1,0:T(8,128)(2,1)S(1)}, bf16[1024,2048]{1,0:T(8,128)(2,1)}, u32[]{:S(2)}) copy-start(bf16[1024,2048]{1,0:T(8,128)(2,1)} %get-tuple-element.8) | copy-start | bytes 12582916
  96.1 4.6 %copy-start.3 = (bf16[1024,2048]{1,0:T(8,128)(2,1)S(1)}, bf16[1024,2048]{1,0:T(8,128)(2,1)}, u32[]{:S(2)}) copy-start(bf16[1024,2048]{1,0:T(8,128)(2,1)} %get-tuple-element.11) | copy-start | bytes 12582916
  100.6 2.4 %copy-start = (bf16[1024,2048]{1,0:T(8,128)(2,1)S(1)}, bf16[1024,2048]{1,0:T(8,128)(2,1)}, u32[]{:S(2)}) copy-start(bf16[1024,2048]{1,0:T(8,128)(2,1)} %get-tuple-element.9) | copy-start | bytes 12582916
  100.7 3.5 %copy-start.1 = (bf16[1024,2048]{1,0:T(8,128)(2,1)S(1)}, bf16[1024,2048]{1,0:T(8,128)(2,1)}, u32[]{:S(2)}) copy-start(bf16[1024,2048]{1,0:T(8,128)(2,1)} %get-tuple-element.10) | copy-start | bytes 12582916
where the time goes:
time: 186 us; the launch traced here: 183 us
  other arithmetic  76.7 us (41%)
  blocking collectives  48.4 us (26%)
  local copies, waits for them, and re-layouts  25.8 us (14%)
  matrix products  17.1 us (9%)
  starting transfers between devices  14.4 us (8%)
    another operation x1, other arithmetic  74.2 us
    all_to_all x1, blocking collectives, per_device(): lax.all_to_all(power_local, 'gx', split_axis=1, concat_axis=0, tiled=True)  27.7 us
    all_to_all x1, blocking collectives, per_device(): lax.all_to_all(lax.all_to_all(power_local, 'gx', split_axis=1, concat_axi...  20.7 us
    all_to_all x1, starting transfers between devices, per_device(): lax.all_to_all(voltages, 'gx', split_axis=2, concat_axis=1, tiled=True)  14.4 us
    reshape x1, local copies, waits for them, and re-layouts, per_device(): power = power.reshape(beam_local, TOUT, total_chans * UPCHAN)  9.89 us
    unnamed x15, local copies, waits for them, and re-layouts  7.39 us
    dot_general x2, matrix products, per_device(): jnp.dot(weight_stacks[which], piece[1, :, which, :], preferred_element_ty...  6.92 us
    dot_general x2, matrix products, per_device(): jnp.dot(weight_stacks[which], piece[0, :, which, :], preferred_element_ty...  4.75 us
  transfers between devices with their start and end apart: 1, of which 0 were waited for; matrix products, arithmetic and copies ran while one was open for 41% of the time, Pallas kernels for 0%

commit v1 on v0

v1 whole, which is shorter than its diff:
```python
import math

import jax
import jax.numpy as jnp
import numpy as np
from jax import lax
from jax.experimental import pallas as pl
from jax.experimental.pallas import tpu as pltpu
from jax.sharding import PartitionSpec as P

FEEDS = 2048
BEAMS = 1024
UPCHAN = 16
TOUT = 8
TIME = 128
F32 = jnp.float32
BF16 = jnp.bfloat16


def fit(values, degree):
    cheb = np.polynomial.Chebyshev.interpolate(values, degree, domain=[0.0, 0.25])
    return [float(c) for c in cheb.convert(kind=np.polynomial.Polynomial).coef]


COS = fit(lambda u: np.cos(2 * np.pi * np.sqrt(u)), 6)
SIN = fit(lambda u: 2 * np.pi * np.sinc(2 * np.sqrt(u)), 6)


def onehot(size, source_of):
    row = lax.broadcasted_iota(jnp.int32, (size, size), 0)
    col = lax.broadcasted_iota(jnp.int32, (size, size), 1)
    return (col == source_of(row)).astype(F32).astype(BF16)


def regroup_kernel(v_ref, out_ref):
    perm = onehot(256, lambda r: (r & 15) * 16 + (r >> 4))
    for f in range(0, v_ref.shape[1], 16):
        rows = jnp.concatenate(
            [v_ref[part, f : f + 16].reshape(256, TIME) for part in range(2)], 1
        )
        moved = jnp.dot(perm, rows, preferred_element_type=F32).astype(BF16)
        for part in range(2):
            out_ref[:, part, f : f + 16, :] = moved[:, part * TIME : (part + 1) * TIME].reshape(
                16, 16, TIME
            )


def regroup(v):
    _, feeds, chans, time = v.shape
    return pl.pallas_call(
        regroup_kernel,
        grid=(chans // 16,),
        in_specs=[pl.BlockSpec((2, feeds, 16, time), lambda i: (0, 0, i, 0))],
        out_specs=pl.BlockSpec((16, 2, feeds, time), lambda i: (i, 0, 0, 0)),
        out_shape=jax.ShapeDtypeStruct((chans, 2, feeds, time), BF16),
        name="regroup",
    )(v)


def weights_kernel(chan_ref, beam_ref, feed_ref, out_ref, turns_ref):
    factor = (chan_ref[0] + pl.program_id(0) + 400) % 4096
    bm = beam_ref.shape[1]

    def rows_of(ref):
        row = lax.broadcasted_iota(jnp.int32, (16, ref.shape[1]), 0)
        return row, jnp.where(row < 2, ref[0:1, :], ref[1:2, :])

    row, grid = rows_of(beam_ref)
    part = (grid * factor) & 4095
    left = jnp.where((row & 1) == 0, part & 4032, part & 63)
    left = jnp.where(row < 4, left, 0).astype(F32).astype(BF16)
    right = rows_of(feed_ref)[1].astype(F32).astype(BF16)
    turns_ref[...] = lax.dot_general(
        left, right, (((0,), (0,)), ((), ())), preferred_element_type=F32
    )
    scale = 1.0 / math.sqrt(FEEDS)
    width = 512

    def chunk(i, carry):
        r0 = pl.multiple_of(i * 16, 16)
        for c0 in range(0, FEEDS, width):
            t = turns_ref[pl.ds(r0, 16), c0 : c0 + width] * (1.0 / 4096.0)
            r = t - jnp.round(t)
            u = r * r
            c = COS[-1] * scale
            for coef in COS[-2::-1]:
                c = c * u + coef * scale
            s = -SIN[-1] * scale
            for coef in SIN[-2::-1]:
                s = s * u - coef * scale
            out_ref[0, pl.ds(r0, 16), c0 : c0 + width] = c.astype(BF16)
            out_ref[0, pl.ds(r0, 16), FEEDS + c0 : FEEDS + c0 + width] = (s * r).astype(BF16)
        return carry

    lax.fori_loop(0, bm // 16, chunk, 0)


def weights(first_chan, beam_grid, feed_pos, local_chans):
    bm = 128
    return pl.pallas_call(
        weights_kernel,
        grid=(local_chans, BEAMS // bm),
        in_specs=[
            pl.BlockSpec(memory_space=pltpu.SMEM),
            pl.BlockSpec((2, bm), lambda c, m: (0, m)),
            pl.BlockSpec((2, FEEDS), lambda c, m: (0, 0)),
        ],
        out_specs=pl.BlockSpec((1, bm, 2 * FEEDS), lambda c, m: (c, m, 0)),
        out_shape=jax.ShapeDtypeStruct((local_chans, BEAMS, 2 * FEEDS), BF16),
        scratch_shapes=[pltpu.VMEM((bm, FEEDS), F32)],
        compiler_params=pltpu.CompilerParams(vmem_limit_bytes=24 * 2**20),
        cost_estimate=pl.CostEstimate(
            flops=30 * local_chans * BEAMS * FEEDS * 20,
            bytes_accessed=local_chans * BEAMS * FEEDS * 4,
            transcendentals=0,
        ),
        name="weights",
    )(first_chan, beam_grid.T, feed_pos.T)


def split(x):
    high = x.astype(BF16)
    return high, (x - high.astype(F32)).astype(BF16)


def beams_kernel(w_ref, v_ref, table_ref, flags_ref, out_ref, rhs_ref, inten_ref, sum_ref, power_ref):
    chan, step = pl.program_id(0), pl.program_id(1)
    bm = w_ref.shape[1]

    @pl.when(step == 0)
    def _():
        real = v_ref[:, chan, 0].reshape(FEEDS, TIME)
        imag = v_ref[:, chan, 1].reshape(FEEDS, TIME)
        rhs_ref[:FEEDS, :TIME] = real
        rhs_ref[:FEEDS, TIME:] = imag
        rhs_ref[FEEDS:, :TIME] = -imag
        rhs_ref[FEEDS:, TIME:] = real
        sum_ref[...] = jnp.zeros_like(sum_ref)

    beam = jnp.dot(w_ref[0], rhs_ref[...], preferred_element_type=F32)
    high, low = split(beam)
    size = 2 * TIME
    fine = (
        jnp.dot(high, table_ref[:size], preferred_element_type=F32)
        + jnp.dot(high, table_ref[size:], preferred_element_type=F32)
        + jnp.dot(low, table_ref[:size], preferred_element_type=F32)
    )
    real, imag = fine[:, :TIME], fine[:, TIME:]
    intensity = real * real + imag * imag
    inten_ref[pl.ds(pl.multiple_of(step * bm, bm), bm), :] = intensity
    sum_ref[...] += jnp.sum(intensity.reshape(bm // 8, 8, TIME), axis=0)

    @pl.when(step == pl.num_programs(1) - 1)
    def _():
        total = jnp.broadcast_to(jnp.sum(sum_ref[...], axis=0, keepdims=True), (8, TIME))
        for shift in (64, 32, 16):
            total = total + pltpu.roll(total, shift, 1)
        bandpass = total[0:1] * (1.0 / (BEAMS * TOUT)) + 1e-06
        scale = flags_ref[pl.ds(chan, 1), :] / bandpass
        power_ref[chan] = (inten_ref[...] * scale).astype(BF16)

    @pl.when((step == pl.num_programs(1) - 1) & (chan == 1))
    def _():
        perm = onehot(256, lambda r: ((r >> 1) & 1) * 128 + (r >> 2) * 2 + (r & 1))
        for i in range(BEAMS // 128):
            pair = power_ref[:, i * 128 : (i + 1) * 128, :].reshape(256, TIME)
            out_ref[i * 256 : (i + 1) * 256, :] = jnp.dot(
                perm, pair, preferred_element_type=F32
            ).astype(BF16)


def dft_table():
    n = np.arange(TIME)
    same = n[:, None] // UPCHAN == n[None, :] // UPCHAN
    angle = 2 * np.pi * ((n[:, None] * n[None, :]) % UPCHAN) / UPCHAN
    cos, sin = np.cos(angle) * same / 4.0, np.sin(angle) * same / 4.0
    table = np.block([[cos, -sin], [sin, cos]]).astype(np.float32)
    high = table.astype(jnp.bfloat16)
    low = (table - high.astype(np.float32)).astype(jnp.bfloat16)
    return np.concatenate([high, low], 0)


def form_beams(w, v, flags):
    bm = 256
    return pl.pallas_call(
        beams_kernel,
        grid=(2, BEAMS // bm),
        in_specs=[
            pl.BlockSpec((1, bm, 2 * FEEDS), lambda c, m: (c, m, 0)),
            pl.BlockSpec(v.shape, lambda c, m: (0, 0, 0, 0, 0)),
            pl.BlockSpec((4 * TIME, 2 * TIME), lambda c, m: (0, 0)),
            pl.BlockSpec((2, TIME), lambda c, m: (0, 0)),
        ],
        out_specs=pl.BlockSpec((2 * BEAMS, TIME), lambda c, m: (0, 0)),
        out_shape=jax.ShapeDtypeStruct((2 * BEAMS, TIME), BF16),
        scratch_shapes=[
            pltpu.VMEM((2 * FEEDS, 2 * TIME), BF16),
            pltpu.VMEM((BEAMS, TIME), F32),
            pltpu.VMEM((8, TIME), F32),
            pltpu.VMEM((2, BEAMS, TIME), BF16),
        ],
        compiler_params=pltpu.CompilerParams(vmem_limit_bytes=32 * 2**20),
        name="beams",
    )(w, v, jnp.asarray(dft_table()), flags)


def finish_kernel(in_ref, power_ref, sums_ref):
    def gather_from(r):
        combo = (r >> 6) * 8 + (r & 7)
        eighth = (r >> 3) & 7
        return (eighth >> 1) * 64 + (combo >> 1) * 4 + (eighth & 1) * 2 + (combo & 1)

    def scatter_from(r):
        combo = r >> 3
        return (combo >> 3) * 64 + (r & 7) * 8 + (combo & 7)

    first, second = onehot(256, gather_from), onehot(256, scatter_from)
    lane = lax.broadcasted_iota(jnp.int32, (8, TIME), 1)
    for q in range(8):
        x = jnp.dot(first, in_ref[q * 256 : (q + 1) * 256, :], preferred_element_type=F32)
        blocks = []
        for group in range(4):
            tiles = [x[group * 64 + i * 8 : group * 64 + i * 8 + 8, :] for i in range(8)]
            for bit in (1, 2, 4):
                upper = (lane & (16 * bit)) != 0
                for i in range(8):
                    if i & bit == 0:
                        low, high = tiles[i], tiles[i | bit]
                        tiles[i] = jnp.where(upper, pltpu.roll(high, 16 * bit, 1), low)
                        tiles[i | bit] = jnp.where(upper, high, pltpu.roll(low, TIME - 16 * bit, 1))
            total = sum(tiles[1:], tiles[0])
            squares = sum([t * t for t in tiles[1:]], tiles[0] * tiles[0])
            for member in range(4):
                gy = group * 4 + member
                at = (gy * 8 + q) * TIME
                sums_ref[0, :, at : at + TIME] = total[2 * member : 2 * member + 2, :]
                sums_ref[1, :, at : at + TIME] = squares[2 * member : 2 * member + 2, :]
            blocks += tiles
        y = jnp.concatenate(blocks, 0).astype(BF16)
        z = jnp.dot(second, y, preferred_element_type=F32).astype(BF16)
        for gy in range(16):
            at = (gy * 8 + q) * TIME
            for beam in range(2):
                row = gy * 16 + beam * 8
                power_ref[beam, :, at : at + TIME] = z[row : row + 8, :]


def finish(received):
    freqs = 512 * 2 * UPCHAN
    return pl.pallas_call(
        finish_kernel,
        out_shape=(
            jax.ShapeDtypeStruct((2, TOUT, freqs), BF16),
            jax.ShapeDtypeStruct((2, 2, freqs), F32),
        ),
        compiler_params=pltpu.CompilerParams(vmem_limit_bytes=24 * 2**20),
        name="finish",
    )(received)


def per_device(voltages, beam_grid, feed_pos, rfi_mask):
    inputs = lax.axis_size("gx")
    chan_dev = voltages.shape[2]
    local_chans = chan_dev // inputs
    first_chan = lax.axis_index("gy") * chan_dev + lax.axis_index("gx") * local_chans
    sent = regroup(voltages)
    piece = lax.all_to_all(sent, "gx", split_axis=0, concat_axis=0, tiled=True)
    w = weights(first_chan.reshape(1).astype(jnp.int32), beam_grid, feed_pos, local_chans)
    flags = rfi_mask.reshape(TOUT, local_chans, UPCHAN).transpose(1, 0, 2).astype(F32)
    piece = piece.reshape(inputs, local_chans, 2, voltages.shape[1], TIME)
    power = form_beams(w, piece, flags.reshape(local_chans, TIME))
    power = power.reshape(512, 4, TIME)
    power = lax.all_to_all(power, ("gx", "gy"), split_axis=0, concat_axis=0, tiled=True)
    return finish(power.reshape(2048, TIME))


def solution(mesh):
    in_specs = (P(None, "gx", "gy", None), P(), P(), P(None, ("gy", "gx")))
    out_specs = (P(("gx", "gy"), None, None), P(None, ("gx", "gy"), None))
    return jax.shard_map(
        per_device, mesh=mesh, in_specs=in_specs, out_specs=out_specs, check_vma=False
    )
```

time: 186 us -> 124 us (0.67); the launches traced: 183 us -> 124 us
  other arithmetic: 76.7 us -> 0.01 us
  Pallas kernels: 0 us -> 39.9 us
  waiting for transfers between devices: 0.01 us -> 22.2 us
  matrix products: 17.1 us -> 0 us
  local copies, waits for them, and re-layouts: 25.8 us -> 11.7 us
  blocking collectives: 48.4 us -> 34.6 us
    another operation x5 -> x0, other arithmetic: 75.4 us -> none
    pallas_call x0 -> x4, Pallas kernels: none -> 39.9 us  [the longest x1 22.8 us: weights(): pl.pallas_call(weights_kernel, grid=(local_chans, BEAMS // bm), in_specs=...]
    all_to_all x1, waiting for transfers between devices: 0.01 us -> 22.2 us  [per_device(): piece = lax.all_to_all(sent, 'gx', split_axis=0, concat_axis=0, tiled=True)]
    dot_general x8 -> x0, matrix products: 17.1 us -> none  [the longest x2 6.92 us: per_device(): jnp.dot(weight_stacks[which], piece[1, :, which, :], preferred_element_ty...]
    all_to_all x2 -> x1, blocking collectives: 48.4 us -> 34.6 us  [per_device(): lax.all_to_all(power, ('gx', 'gy'), split_axis=0, concat_axis=0, tiled=True)]
    reshape x3 -> x1, local copies, waits for them, and re-layouts: 11.5 us -> 0.08 us  [per_device(): power = form_beams(w, piece, flags.reshape(local_chans, TIME))]
    unnamed x15 -> x12, local copies, waits for them, and re-layouts: 7.39 us -> 11.5 us
    transpose x1 -> x0, local copies, waits for them, and re-layouts: 3.11 us -> none  [per_device(): gathered.reshape(total_chans, beam_local, TOUT, UPCHAN)]
  transfers between devices with their start and end apart: 1 -> 1, of which waited for: 0 -> 1; matrix products, arithmetic and copies ran while one was open for 41% -> 0% of each run, Pallas kernels for 0% -> 18%
where the time goes in v1:
time: 124 us
  Pallas kernels  39.9 us (32%)
  blocking collectives  34.6 us (28%)
  waiting for transfers between devices  22.2 us (18%)
  starting transfers between devices  14.6 us (12%)
  local copies, waits for them, and re-layouts  11.7 us (9%)
    all_to_all x1, blocking collectives, per_device(): lax.all_to_all(power, ('gx', 'gy'), split_axis=0, concat_axis=0, tiled=True)  34.6 us
    pallas_call x1, Pallas kernels, weights(): pl.pallas_call(weights_kernel, grid=(local_chans, BEAMS // bm), in_specs=...  22.8 us
    all_to_all x1, waiting for transfers between devices, per_device(): piece = lax.all_to_all(sent, 'gx', split_axis=0, concat_axis=0, tiled=True)  22.2 us
    all_to_all x1, starting transfers between devices, per_device(): piece = lax.all_to_all(sent, 'gx', split_axis=0, concat_axis=0, tiled=True)  14.6 us
    unnamed x12, local copies, waits for them, and re-layouts  11.5 us
    pallas_call x1, Pallas kernels, form_beams(): pl.pallas_call(beams_kernel, grid=(2, BEAMS // bm), in_specs=[pl.BlockSpe...  10.6 us
    pallas_call x1, Pallas kernels, regroup(): pl.pallas_call(regroup_kernel, grid=(chans // 16,), in_specs=[pl.BlockSpe...  4.37 us
  transfers between devices with their start and end apart: 1, of which 1 were waited for; matrix products, arithmetic and copies ran while one was open for 0% of the time, Pallas kernels for 18%

profile of v1, /device:TPU:1, one launch (start us, length us, event | category | flops | bytes accessed | tf_op | source)
XLA Modules:
  0.0 123.6 jit_solution(10594393525208635448)
XLA Ops:
  0.6 4.4 %regroup.1 = bf16[64,2,64,128]{3,2,1,0:T(8,128)(2,1)} custom-call(bf16[2,64,64,128]{3,2,1,0:T(8,128)(2,1)} %v_ref.1), custom_call_target="tpu_custom_call" | custom-call | tf_op jit(solution)/shard_map/regroup/pallas_call | solution.py:50
  5.0 0.0 copy-start.5
  5.0 0.0 copy-start.3
  5.0 0.0 copy-start.4
  5.0 14.6 %all-to-all-start = ((bf16[64,2,64,128]{3,2,1,0:T(8,128)(2,1)}), bf16[64,2,64,128]{3,2,1,0:T(8,128)(2,1)S(1)}, u32[]{:S(2)}, u32[]{:S(2)}) async-start(bf16[64,2,64,128]{3,2,1,0:T(8,128)(2,1)} %regroup.1), calls=%async_computation | async-start | bytes 4194304 | tf_op jit(solution)/shard_map/all_to_all | solution.py:267
  19.6 0.0 copy-done.5
  19.6 0.1 convert_element_type.10
  19.7 0.1 reshape.23.flags_ref
  19.8 0.0 copy-done.3
  19.8 0.0 copy-done.4
  19.8 0.0 copy-start.2
  19.8 22.8 %weights.1.w_ref = bf16[2,1024,4096]{2,1,0:T(8,128)(2,1)S(1)} custom-call(s32[1]{0:T(128)} %bitcast.chan_ref, s32[2,1024]{1,0:T(2,128)S(1)} %bitcast.13, s32[2,2048]{1,0:T(2,128)S(1)} %bitcast.12), custom_call_target="tpu_custom_call" | custom-call | flops 2516582400 | bytes 16777216 | tf_op jit(solution)/shard_map/weights/pallas_call | solution.py:100
  42.6 0.0 copy-start
  42.6 5.7 %copy-done = bf16[2,1024,4096]{2,1,0:T(8,128)(2,1)} copy-done((bf16[2,1024,4096]{2,1,0:T(8,128)(2,1)}, bf16[2,1024,4096]{2,1,0:T(8,128)(2,1)S(1)}, u32[]{:S(2)}) %copy-start) | copy-done | bytes 16777240
  48.3 22.2 %all-to-all-done = bf16[64,2,64,128]{3,2,1,0:T(8,128)(2,1)S(1)} async-done(((bf16[64,2,64,128]{3,2,1,0:T(8,128)(2,1)}), bf16[64,2,64,128]{3,2,1,0:T(8,128)(2,1)S(1)}, u32[]{:S(2)}, u32[]{:S(2)}) %all-to-all-start) | async-done | bytes 2097184 | tf_op jit(solution)/shard_map/all_to_all | solution.py:267
  70.5 0.0 copy-done.2
  70.5 0.0 copy-start.1
  70.5 5.8 %copy-done.1 = bf16[2,1024,4096]{2,1,0:T(8,128)(2,1)S(1)} copy-done((bf16[2,1024,4096]{2,1,0:T(8,128)(2,1)S(1)}, bf16[2,1024,4096]{2,1,0:T(8,128)(2,1)}, u32[]{:S(2)}) %copy-start.1) | copy-done | bytes 16777240
  76.3 10.6 %beams.1 = bf16[2048,128]{1,0:T(8,128)(2,1)S(1)} custom-call(bf16[2,1024,4096]{2,1,0:T(8,128)(2,1)S(1)} %copy-done.1, bf16[32,2,2,64,128]{4,3,2,1,0:T(8,128)(2,1)S(1)} %bitcast.9, bf16[512,256]{1,0:T(8,128)(2,1)S(1)} %copy-done.2, f32[2,128]{1,0:T(2,128)S(1)} %reshape.23.flags_ref), custom_call_target="tpu_custom_call" | custom-call | tf_op jit(solution)/shard_map/beams/pallas_call | solution.py:185
  86.8 34.6 %all_to_all.10 = bf16[512,4,128]{2,1,0:T(4,128)(2,1)S(1)} all-to-all(bf16[512,4,128]{2,1,0:T(4,128)(2,1)S(1)} %bitcast.10), channel_id=1, replica_groups=mesh['gx'=32,'gy'=16] {'gx','gy'}, dimensions={0} | all-to-all | bytes 1048576 | tf_op jit(solution)/shard_map/all_to_all | solution.py:273
  121.4 2.2 %finish.1 = (bf16[2,8,16384]{2,1,0:T(8,128)(2,1)}, f32[2,2,16384]{2,1,0:T(2,128)}) custom-call(bf16[2048,128]{1,0:T(8,128)(2,1)S(1)} %bitcast.11), custom_call_target="tpu_custom_call" | custom-call | tf_op jit(solution)/shard_map/finish/pallas_call | solution.py:250
  (2 shorter events, 0.0 us)
Async XLA Ops:
  5.0 14.6 %copy-start.5 = (s32[8,32]{1,0:T(8,128)S(1)}, s32[8,32]{1,0:T(8,128)}, u32[]{:S(2)}) copy-start(s32[8,32]{1,0:T(8,128)} %param.8) | copy-start | bytes 3076
  5.0 14.8 %copy-start.3 = (s32[2048,2]{0,1:T(2,128)S(1)}, s32[2048,2]{0,1:T(2,128)}, u32[]{:S(2)}) copy-start(s32[2048,2]{0,1:T(2,128)} %param.7) | copy-start | bytes 49156
  5.0 14.8 %copy-start.4 = (s32[1024,2]{0,1:T(2,128)S(1)}, s32[1024,2]{0,1:T(2,128)}, u32[]{:S(2)}) copy-start(s32[1024,2]{0,1:T(2,128)} %param.6) | copy-start | bytes 24580
  5.0 65.5 %all-to-all-start = ((bf16[64,2,64,128]{3,2,1,0:T(8,128)(2,1)}), bf16[64,2,64,128]{3,2,1,0:T(8,128)(2,1)S(1)}, u32[]{:S(2)}, u32[]{:S(2)}) async-start(bf16[64,2,64,128]{3,2,1,0:T(8,128)(2,1)} %regroup.1), calls=%async_computation | async-start | bytes 4194304 | tf_op jit(solution)/shard_map/all_to_all | solution.py:267
  19.8 50.7 %copy-start.2 = (bf16[512,256]{1,0:T(8,128)(2,1)S(1)}, bf16[512,256]{1,0:T(8,128)(2,1)}, u32[]{:S(2)}) copy-start(bf16[512,256]{1,0:T(8,128)(2,1)} %constant.15.clone.table_ref) | copy-start | bytes 786436
  42.6 5.7 %copy-start = (bf16[2,1024,4096]{2,1,0:T(8,128)(2,1)}, bf16[2,1024,4096]{2,1,0:T(8,128)(2,1)S(1)}, u32[]{:S(2)}) copy-start(bf16[2,1024,4096]{2,1,0:T(8,128)(2,1)S(1)} %weights.1.w_ref) | copy-start | bytes 50331652
  70.5 5.8 %copy-start.1 = (bf16[2,1024,4096]{2,1,0:T(8,128)(2,1)S(1)}, bf16[2,1024,4096]{2,1,0:T(8,128)(2,1)}, u32[]{:S(2)}) copy-start(bf16[2,1024,4096]{2,1,0:T(8,128)(2,1)} %copy-done) | copy-start | bytes 50331652

commit v2 on v1

--- a/solution.py
+++ b/solution.py
@@ -32,29 +32,47 @@
     return (col == source_of(row)).astype(F32).astype(BF16)
 
 
-def regroup_kernel(v_ref, out_ref):
-    perm = onehot(256, lambda r: (r & 15) * 16 + (r >> 4))
-    for f in range(0, v_ref.shape[1], 16):
-        rows = jnp.concatenate(
-            [v_ref[part, f : f + 16].reshape(256, TIME) for part in range(2)], 1
-        )
-        moved = jnp.dot(perm, rows, preferred_element_type=F32).astype(BF16)
-        for part in range(2):
-            out_ref[:, part, f : f + 16, :] = moved[:, part * TIME : (part + 1) * TIME].reshape(
-                16, 16, TIME
-            )
+def regroup_kernel(v_ref, out_ref, in_buf, out_buf, in_sem, out_sem):
+    parts, feeds, chans, _ = v_ref.shape
+    pieces = [(part, f) for f in range(0, feeds, 16) for part in range(parts)]
+
+    def fetch(n):
+        at = (pieces[n][0], pl.ds(pieces[n][1], 16))
+        return pltpu.make_async_copy(v_ref.at[at], in_buf.at[at], in_sem.at[n])
+
+    def store(n):
+        at = (slice(None), pieces[n][0], pl.ds(pieces[n][1], 16))
+        return pltpu.make_async_copy(out_buf.at[at], out_ref.at[at], out_sem.at[n])
+
+    for n in range(len(pieces)):
+        fetch(n).start()
+    for n, (part, f) in enumerate(pieces):
+        fetch(n).wait()
+        for c in range(0, chans, 16):
+            tile = in_buf[part, f : f + 16, c : c + 16]
+            out_buf[c : c + 16, part, f : f + 16, :] = jnp.swapaxes(tile, 0, 1)
+        store(n).start()
+    for n in range(len(pieces)):
+        store(n).wait()
 
 
 def regroup(v):
-    _, feeds, chans, time = v.shape
+    parts, feeds, chans, time = v.shape
+    count = parts * feeds // 16
     return pl.pallas_call(
         regroup_kernel,
-        grid=(chans // 16,),
-        in_specs=[pl.BlockSpec((2, feeds, 16, time), lambda i: (0, 0, i, 0))],
-        out_specs=pl.BlockSpec((16, 2, feeds, time), lambda i: (i, 0, 0, 0)),
-        out_shape=jax.ShapeDtypeStruct((chans, 2, feeds, time), BF16),
+        in_specs=[pl.BlockSpec(memory_space=pltpu.HBM)],
+        out_specs=pl.BlockSpec(memory_space=pltpu.HBM),
+        out_shape=jax.ShapeDtypeStruct((chans, parts, feeds, time), BF16),
+        scratch_shapes=[
+            pltpu.VMEM(v.shape, BF16),
+            pltpu.VMEM((chans, parts, feeds, time), BF16),
+            pltpu.SemaphoreType.DMA((count,)),
+            pltpu.SemaphoreType.DMA((count,)),
+        ],
+        compiler_params=pltpu.CompilerParams(vmem_limit_bytes=16 * 2**20),
         name="regroup",
-    )(v)
+    )(pltpu.with_memory_space_constraint(v, pltpu.HBM))
 
 
 def weights_kernel(chan_ref, beam_ref, feed_ref, out_ref, turns_ref):
@@ -106,7 +124,7 @@
             pl.BlockSpec((2, FEEDS), lambda c, m: (0, 0)),
         ],
         out_specs=pl.BlockSpec((1, bm, 2 * FEEDS), lambda c, m: (c, m, 0)),
-        out_shape=jax.ShapeDtypeStruct((local_chans, BEAMS, 2 * FEEDS), BF16),
+        out_shape=pltpu.HBM((local_chans, BEAMS, 2 * FEEDS), BF16),
         scratch_shapes=[pltpu.VMEM((bm, FEEDS), F32)],
         compiler_params=pltpu.CompilerParams(vmem_limit_bytes=24 * 2**20),
         cost_estimate=pl.CostEstimate(
@@ -123,50 +141,81 @@
     return high, (x - high.astype(F32)).astype(BF16)
 
 
-def beams_kernel(w_ref, v_ref, table_ref, flags_ref, out_ref, rhs_ref, inten_ref, sum_ref, power_ref):
-    chan, step = pl.program_id(0), pl.program_id(1)
-    bm = w_ref.shape[1]
-
-    @pl.when(step == 0)
-    def _():
+def beams_kernel(
+    w_hbm, v_ref, table_ref, flags_ref, out_ref, w_buf, sem, rhs_ref, beam_ref, inten_ref, rows_ref
+):
+    slots, bm, _ = w_buf.shape
+    steps = BEAMS // bm
+    size = 2 * TIME
+
+    def fetch(i):
+        rows = pl.ds(pl.multiple_of(i % steps * bm, bm), bm)
+        return pltpu.make_async_copy(w_hbm.at[i // steps, rows], w_buf.at[i % slots], sem.at[i % slots])
+
+    for i in range(slots):
+        fetch(i).start()
+    for chan in range(2):
         real = v_ref[:, chan, 0].reshape(FEEDS, TIME)
         imag = v_ref[:, chan, 1].reshape(FEEDS, TIME)
-        rhs_ref[:FEEDS, :TIME] = real
-        rhs_ref[:FEEDS, TIME:] = imag
-        rhs_ref[FEEDS:, :TIME] = -imag
-        rhs_ref[FEEDS:, TIME:] = real
-        sum_ref[...] = jnp.zeros_like(sum_ref)
-
-    beam = jnp.dot(w_ref[0], rhs_ref[...], preferred_element_type=F32)
-    high, low = split(beam)
-    size = 2 * TIME
-    fine = (
-        jnp.dot(high, table_ref[:size], preferred_element_type=F32)
-        + jnp.dot(high, table_ref[size:], preferred_element_type=F32)
-        + jnp.dot(low, table_ref[:size], preferred_element_type=F32)
-    )
-    real, imag = fine[:, :TIME], fine[:, TIME:]
-    intensity = real * real + imag * imag
-    inten_ref[pl.ds(pl.multiple_of(step * bm, bm), bm), :] = intensity
-    sum_ref[...] += jnp.sum(intensity.reshape(bm // 8, 8, TIME), axis=0)
-
-    @pl.when(step == pl.num_programs(1) - 1)
-    def _():
-        total = jnp.broadcast_to(jnp.sum(sum_ref[...], axis=0, keepdims=True), (8, TIME))
+        rhs_ref[chan, :FEEDS, :TIME] = real
+        rhs_ref[chan, :FEEDS, TIME:] = imag
+        rhs_ref[chan, FEEDS:, :TIME] = -imag
+        rhs_ref[chan, FEEDS:, TIME:] = real
+    beam_ref[1] = jnp.zeros_like(beam_ref[1])
+
+    def detect(i):
+        high, low = split(beam_ref[i % 2])
+        fine = (
+            jnp.dot(high, table_ref[:size], preferred_element_type=F32)
+            + jnp.dot(high, table_ref[size:], preferred_element_type=F32)
+            + jnp.dot(low, table_ref[:size], preferred_element_type=F32)
+        )
+        real, imag = fine[:, :TIME], fine[:, TIME:]
+        rows = pl.ds(pl.multiple_of(i % steps * bm, bm), bm)
+        inten_ref[i // steps, rows, :] = real * real + imag * imag
+
+    def normalize(chan):
+        def add(j, total):
+            x = inten_ref[chan, pl.ds(pl.multiple_of(j * 128, 128), 128), :]
+            return total + jnp.sum(x.reshape(16, 8, TIME), axis=0)
+
+        total = lax.fori_loop(0, BEAMS // 128, add, jnp.zeros((8, TIME), F32))
+        total = jnp.broadcast_to(jnp.sum(total, axis=0, keepdims=True), (8, TIME))
         for shift in (64, 32, 16):
             total = total + pltpu.roll(total, shift, 1)
         bandpass = total[0:1] * (1.0 / (BEAMS * TOUT)) + 1e-06
-        scale = flags_ref[pl.ds(chan, 1), :] / bandpass
-        power_ref[chan] = (inten_ref[...] * scale).astype(BF16)
-
-    @pl.when((step == pl.num_programs(1) - 1) & (chan == 1))
-    def _():
-        perm = onehot(256, lambda r: ((r >> 1) & 1) * 128 + (r >> 2) * 2 + (r & 1))
-        for i in range(BEAMS // 128):
-            pair = power_ref[:, i * 128 : (i + 1) * 128, :].reshape(256, TIME)
-            out_ref[i * 256 : (i + 1) * 256, :] = jnp.dot(
-                perm, pair, preferred_element_type=F32
-            ).astype(BF16)
+        scale = flags_ref[chan : chan + 1, :] / bandpass
+
+        def move(j, carry):
+            for beam in range(2):
+                x = inten_ref[chan, pl.ds(j * 128 + beam, 64, stride=2), :]
+                rows_ref[pl.ds(j * 256 + 2 * chan + beam, 64, stride=4), :] = x * scale
+            if chan == 1:
+                rows = pl.ds(pl.multiple_of(j * 256, 256), 256)
+                out_ref[rows, :] = rows_ref[rows, :].astype(BF16)
+            return carry
+
+        lax.fori_loop(0, BEAMS // 128, move, 0)
+
+    def body(i, carry):
+        fetch(i).wait()
+        beam = jnp.dot(w_buf[i % slots], rhs_ref[i // steps], preferred_element_type=F32)
+        detect(jnp.maximum(i - 1, 0))
+        beam_ref[i % 2] = beam
+
+        @pl.when(i + slots < 2 * steps)
+        def _():
+            fetch(i + slots).start()
+
+        @pl.when(i == steps)
+        def _():
+            normalize(0)
+
+        return carry
+
+    lax.fori_loop(0, 2 * steps, body, 0)
+    detect(2 * steps - 1)
+    normalize(1)
 
 
 def dft_table():
@@ -181,27 +230,24 @@
 
 
 def form_beams(w, v, flags):
-    bm = 256
+    bm, slots = 256, 4
+    vmem = pl.BlockSpec(memory_space=pltpu.VMEM)
     return pl.pallas_call(
         beams_kernel,
-        grid=(2, BEAMS // bm),
-        in_specs=[
-            pl.BlockSpec((1, bm, 2 * FEEDS), lambda c, m: (c, m, 0)),
-            pl.BlockSpec(v.shape, lambda c, m: (0, 0, 0, 0, 0)),
-            pl.BlockSpec((4 * TIME, 2 * TIME), lambda c, m: (0, 0)),
-            pl.BlockSpec((2, TIME), lambda c, m: (0, 0)),
-        ],
-        out_specs=pl.BlockSpec((2 * BEAMS, TIME), lambda c, m: (0, 0)),
+        in_specs=[pl.BlockSpec(memory_space=pltpu.HBM), vmem, vmem, vmem],
+        out_specs=vmem,
         out_shape=jax.ShapeDtypeStruct((2 * BEAMS, TIME), BF16),
         scratch_shapes=[
-            pltpu.VMEM((2 * FEEDS, 2 * TIME), BF16),
-            pltpu.VMEM((BEAMS, TIME), F32),
-            pltpu.VMEM((8, TIME), F32),
-            pltpu.VMEM((2, BEAMS, TIME), BF16),
+            pltpu.VMEM((slots, bm, 2 * FEEDS), BF16),
+            pltpu.SemaphoreType.DMA((slots,)),
+            pltpu.VMEM((2, 2 * FEEDS, 2 * TIME), BF16),
+            pltpu.VMEM((2, bm, 2 * TIME), F32),
+            pltpu.VMEM((2, BEAMS, TIME), F32),
+            pltpu.VMEM((2 * BEAMS, TIME), F32),
         ],
         compiler_params=pltpu.CompilerParams(vmem_limit_bytes=32 * 2**20),
         name="beams",
-    )(w, v, jnp.asarray(dft_table()), flags)
+    )(pltpu.with_memory_space_constraint(w, pltpu.HBM), v, jnp.asarray(dft_table()), flags)
 
 
 def finish_kernel(in_ref, power_ref, sums_ref):

time: 124 us -> 116 us (0.935)
  local copies, waits for them, and re-layouts: 11.7 us -> 1.53 us
  waiting for transfers between devices: 22.2 us -> 26.7 us
  Pallas kernels: 39.9 us -> 38 us
    unnamed x12 -> x10, local copies, waits for them, and re-layouts: 11.5 us -> 1.36 us
    all_to_all x1, waiting for transfers between devices: 22.2 us -> 26.7 us  [per_device(): piece = lax.all_to_all(sent, 'gx', split_axis=0, concat_axis=0, tiled=True)]
    pallas_call x2, Pallas kernels: 14.9 us -> 11.8 us  [the longest x1 9.46 us: form_beams(): pl.pallas_call(beams_kernel, in_specs=[pl.BlockSpec(memory_space=pltpu.HB...]
    pallas_call x1, Pallas kernels: 22.8 us -> 24 us  [weights(): pl.pallas_call(weights_kernel, grid=(local_chans, BEAMS // bm), in_specs=...]
  transfers between devices with their start and end apart: 1 -> 1, of which waited for: 1 -> 1; matrix products, arithmetic and copies ran while one was open for 0% -> 0% of each run, Pallas kernels for 18% -> 21%
where the time goes in v2:
time: 116 us
  Pallas kernels  38 us (33%)
  blocking collectives  34.6 us (30%)
  waiting for transfers between devices  26.7 us (23%)
  starting transfers between devices  14.6 us (13%)
  local copies, waits for them, and re-layouts  1.53 us (1%)
    all_to_all x1, blocking collectives, per_device(): lax.all_to_all(power, ('gx', 'gy'), split_axis=0, concat_axis=0, tiled=True)  34.6 us
    all_to_all x1, waiting for transfers between devices, per_device(): piece = lax.all_to_all(sent, 'gx', split_axis=0, concat_axis=0, tiled=True)  26.7 us
    pallas_call x1, Pallas kernels, weights(): pl.pallas_call(weights_kernel, grid=(local_chans, BEAMS // bm), in_specs=...  24 us
    all_to_all x1, starting transfers between devices, per_device(): piece = lax.all_to_all(sent, 'gx', split_axis=0, concat_axis=0, tiled=True)  14.6 us
    pallas_call x1, Pallas kernels, form_beams(): pl.pallas_call(beams_kernel, in_specs=[pl.BlockSpec(memory_space=pltpu.HB...  9.46 us
    pallas_call x1, Pallas kernels, regroup(): pl.pallas_call(regroup_kernel, in_specs=[pl.BlockSpec(memory_space=pltpu....  2.33 us
  transfers between devices with their start and end apart: 1, of which 1 were waited for; matrix products, arithmetic and copies ran while one was open for 0% of the time, Pallas kernels for 21%

profile of v2, /device:TPU:1, one launch (start us, length us, event | category | flops | bytes accessed | tf_op | source)
XLA Modules:
  0.0 116.0 jit_solution(8199271046258943184)
XLA Ops:
  0.6 2.3 %regroup.1 = bf16[64,2,64,128]{3,2,1,0:T(8,128)(2,1)S(1)} custom-call(bf16[2,64,64,128]{3,2,1,0:T(8,128)(2,1)} %v_ref.1), custom_call_target="tpu_custom_call" | custom-call | tf_op jit(solution)/shard_map/regroup/pallas_call | solution.py:62
  3.0 0.0 copy-start
  3.0 1.3 %copy-done = bf16[64,2,64,128]{3,2,1,0:T(8,128)(2,1)} copy-done((bf16[64,2,64,128]{3,2,1,0:T(8,128)(2,1)}, bf16[64,2,64,128]{3,2,1,0:T(8,128)(2,1)S(1)}, u32[]{:S(2)}) %copy-start) | copy-done | bytes 2097176
  4.3 0.0 copy-start.4
  4.3 0.0 copy-start.2
  4.3 0.0 copy-start.3
  4.3 14.6 %all-to-all-start = ((bf16[64,2,64,128]{3,2,1,0:T(8,128)(2,1)}), bf16[64,2,64,128]{3,2,1,0:T(8,128)(2,1)S(1)}, u32[]{:S(2)}, u32[]{:S(2)}) async-start(bf16[64,2,64,128]{3,2,1,0:T(8,128)(2,1)} %copy-done), calls=%async_computation | async-start | bytes 4194304 | tf_op jit(solution)/shard_map/all_to_all | solution.py:313
  18.9 0.0 copy-done.4
  18.9 0.1 convert_element_type.10
  19.0 0.1 reshape.23.flags_ref
  19.1 0.0 copy-done.2
  19.1 0.0 copy-done.3
  19.1 0.0 copy-start.1
  19.1 24.0 %weights.1.w_hbm = bf16[2,1024,4096]{2,1,0:T(8,128)(2,1)} custom-call(s32[1]{0:T(128)} %bitcast.chan_ref, s32[2,1024]{1,0:T(2,128)S(1)} %bitcast.13, s32[2,2048]{1,0:T(2,128)S(1)} %bitcast.12), custom_call_target="tpu_custom_call" | custom-call | flops 2516582400 | bytes 16777216 | tf_op jit(solution)/shard_map/weights/pallas_call | solution.py:118
  43.1 26.7 %all-to-all-done = bf16[64,2,64,128]{3,2,1,0:T(8,128)(2,1)S(1)} async-done(((bf16[64,2,64,128]{3,2,1,0:T(8,128)(2,1)}), bf16[64,2,64,128]{3,2,1,0:T(8,128)(2,1)S(1)}, u32[]{:S(2)}, u32[]{:S(2)}) %all-to-all-start) | async-done | bytes 2097184 | tf_op jit(solution)/shard_map/all_to_all | solution.py:313
  69.8 0.0 copy-done.1
  69.8 9.5 %beams.1 = bf16[2048,128]{1,0:T(8,128)(2,1)S(1)} custom-call(bf16[2,1024,4096]{2,1,0:T(8,128)(2,1)} %weights.1.w_hbm, bf16[32,2,2,64,128]{4,3,2,1,0:T(8,128)(2,1)S(1)} %bitcast.9, bf16[512,256]{1,0:T(8,128)(2,1)S(1)} %copy-done.1, f32[2,128]{1,0:T(2,128)S(1)} %reshape.23.flags_ref), custom_call_target="tpu_custom_call" | custom-call | tf_op jit(solution)/shard_map/beams/pallas_call | solution.py:235
  79.3 34.6 %all_to_all.10 = bf16[512,4,128]{2,1,0:T(4,128)(2,1)S(1)} all-to-all(bf16[512,4,128]{2,1,0:T(4,128)(2,1)S(1)} %bitcast.10), channel_id=1, replica_groups=mesh['gx'=32,'gy'=16] {'gx','gy'}, dimensions={0} | all-to-all | bytes 1048576 | tf_op jit(solution)/shard_map/all_to_all | solution.py:319
  113.8 2.2 %finish.1 = (bf16[2,8,16384]{2,1,0:T(8,128)(2,1)}, f32[2,2,16384]{2,1,0:T(2,128)}) custom-call(bf16[2048,128]{1,0:T(8,128)(2,1)S(1)} %bitcast.11), custom_call_target="tpu_custom_call" | custom-call | tf_op jit(solution)/shard_map/finish/pallas_call | solution.py:296
  (2 shorter events, 0.0 us)
Async XLA Ops:
  3.0 1.4 %copy-start = (bf16[64,2,64,128]{3,2,1,0:T(8,128)(2,1)}, bf16[64,2,64,128]{3,2,1,0:T(8,128)(2,1)S(1)}, u32[]{:S(2)}) copy-start(bf16[64,2,64,128]{3,2,1,0:T(8,128)(2,1)S(1)} %regroup.1) | copy-start | bytes 6291460
  4.3 14.6 %copy-start.4 = (s32[8,32]{1,0:T(8,128)S(1)}, s32[8,32]{1,0:T(8,128)}, u32[]{:S(2)}) copy-start(s32[8,32]{1,0:T(8,128)} %param.8) | copy-start | bytes 3076
  4.3 14.8 %copy-start.2 = (s32[2048,2]{0,1:T(2,128)S(1)}, s32[2048,2]{0,1:T(2,128)}, u32[]{:S(2)}) copy-start(s32[2048,2]{0,1:T(2,128)} %param.7) | copy-start | bytes 49156
  4.3 14.8 %copy-start.3 = (s32[1024,2]{0,1:T(2,128)S(1)}, s32[1024,2]{0,1:T(2,128)}, u32[]{:S(2)}) copy-start(s32[1024,2]{0,1:T(2,128)} %param.6) | copy-start | bytes 24580
  4.3 65.5 %all-to-all-start = ((bf16[64,2,64,128]{3,2,1,0:T(8,128)(2,1)}), bf16[64,2,64,128]{3,2,1,0:T(8,128)(2,1)S(1)}, u32[]{:S(2)}, u32[]{:S(2)}) async-start(bf16[64,2,64,128]{3,2,1,0:T(8,128)(2,1)} %copy-done), calls=%async_computation | async-start | bytes 4194304 | tf_op jit(solution)/shard_map/all_to_all | solution.py:313
  19.1 50.7 %copy-start.1 = (bf16[512,256]{1,0:T(8,128)(2,1)S(1)}, bf16[512,256]{1,0:T(8,128)(2,1)}, u32[]{:S(2)}) copy-start(bf16[512,256]{1,0:T(8,128)(2,1)} %constant.15.clone.table_ref) | copy-start | bytes 786436

commit v3 on v2

--- a/solution.py
+++ b/solution.py
@@ -1,3 +1,4 @@
+import functools
 import math
 
 import jax
@@ -63,7 +64,7 @@
         regroup_kernel,
         in_specs=[pl.BlockSpec(memory_space=pltpu.HBM)],
         out_specs=pl.BlockSpec(memory_space=pltpu.HBM),
-        out_shape=jax.ShapeDtypeStruct((chans, parts, feeds, time), BF16),
+        out_shape=pltpu.HBM((chans, parts, feeds, time), BF16),
         scratch_shapes=[
             pltpu.VMEM(v.shape, BF16),
             pltpu.VMEM((chans, parts, feeds, time), BF16),
@@ -75,8 +76,9 @@
     )(pltpu.with_memory_space_constraint(v, pltpu.HBM))
 
 
-def weights_kernel(chan_ref, beam_ref, feed_ref, out_ref, turns_ref):
-    factor = (chan_ref[0] + pl.program_id(0) + 400) % 4096
+def weights_kernel(local_chans, beam_ref, feed_ref, out_ref, turns_ref):
+    device = lax.axis_index("gy") * lax.axis_size("gx") + lax.axis_index("gx")
+    factor = (device * local_chans + pl.program_id(0) + 400) % 4096
     bm = beam_ref.shape[1]
 
     def rows_of(ref):
@@ -113,13 +115,12 @@
     lax.fori_loop(0, bm // 16, chunk, 0)
 
 
-def weights(first_chan, beam_grid, feed_pos, local_chans):
+def weights(beam_grid, feed_pos, local_chans):
     bm = 128
     return pl.pallas_call(
-        weights_kernel,
+        functools.partial(weights_kernel, local_chans),
         grid=(local_chans, BEAMS // bm),
         in_specs=[
-            pl.BlockSpec(memory_space=pltpu.SMEM),
             pl.BlockSpec((2, bm), lambda c, m: (0, m)),
             pl.BlockSpec((2, FEEDS), lambda c, m: (0, 0)),
         ],
@@ -133,7 +134,7 @@
             transcendentals=0,
         ),
         name="weights",
-    )(first_chan, beam_grid.T, feed_pos.T)
+    )(beam_grid.T, feed_pos.T)
 
 
 def split(x):
@@ -142,7 +143,7 @@
 
 
 def beams_kernel(
-    w_hbm, v_ref, table_ref, flags_ref, out_ref, w_buf, sem, rhs_ref, beam_ref, inten_ref, rows_ref
+    w_hbm, v_ref, table_ref, flags_ref, out_ref, w_buf, sem, rhs_ref, beam_ref, inten_ref, rows_ref, sum_ref
 ):
     slots, bm, _ = w_buf.shape
     steps = BEAMS // bm
@@ -172,14 +173,12 @@
         )
         real, imag = fine[:, :TIME], fine[:, TIME:]
         rows = pl.ds(pl.multiple_of(i % steps * bm, bm), bm)
-        inten_ref[i // steps, rows, :] = real * real + imag * imag
+        x = real * real + imag * imag
+        inten_ref[i // steps, rows, :] = x
+        sum_ref[i] = jnp.sum(x.reshape(bm // 8, 8, TIME), axis=0)
 
     def normalize(chan):
-        def add(j, total):
-            x = inten_ref[chan, pl.ds(pl.multiple_of(j * 128, 128), 128), :]
-            return total + jnp.sum(x.reshape(16, 8, TIME), axis=0)
-
-        total = lax.fori_loop(0, BEAMS // 128, add, jnp.zeros((8, TIME), F32))
+        total = jnp.sum(sum_ref[chan * steps : (chan + 1) * steps], axis=0)
         total = jnp.broadcast_to(jnp.sum(total, axis=0, keepdims=True), (8, TIME))
         for shift in (64, 32, 16):
             total = total + pltpu.roll(total, shift, 1)
@@ -195,7 +194,7 @@
                 out_ref[rows, :] = rows_ref[rows, :].astype(BF16)
             return carry
 
-        lax.fori_loop(0, BEAMS // 128, move, 0)
+        lax.fori_loop(0, BEAMS // 128, move, 0, unroll=True)
 
     def body(i, carry):
         fetch(i).wait()
@@ -244,6 +243,7 @@
             pltpu.VMEM((2, bm, 2 * TIME), F32),
             pltpu.VMEM((2, BEAMS, TIME), F32),
             pltpu.VMEM((2 * BEAMS, TIME), F32),
+            pltpu.VMEM((2 * BEAMS // bm, 8, TIME), F32),
         ],
         compiler_params=pltpu.CompilerParams(vmem_limit_bytes=32 * 2**20),
         name="beams",
@@ -308,10 +308,9 @@
     inputs = lax.axis_size("gx")
     chan_dev = voltages.shape[2]
     local_chans = chan_dev // inputs
-    first_chan = lax.axis_index("gy") * chan_dev + lax.axis_index("gx") * local_chans
     sent = regroup(voltages)
     piece = lax.all_to_all(sent, "gx", split_axis=0, concat_axis=0, tiled=True)
-    w = weights(first_chan.reshape(1).astype(jnp.int32), beam_grid, feed_pos, local_chans)
+    w = weights(beam_grid, feed_pos, local_chans)
     flags = rfi_mask.reshape(TOUT, local_chans, UPCHAN).transpose(1, 0, 2).astype(F32)
     piece = piece.reshape(inputs, local_chans, 2, voltages.shape[1], TIME)
     power = form_beams(w, piece, flags.reshape(local_chans, TIME))

time: 116 us -> 115 us (level)
  local copies, waits for them, and re-layouts: 1.53 us -> 0.19 us
    unnamed x10 -> x8, local copies, waits for them, and re-layouts: 1.36 us -> 0.03 us
where the time goes in v3:
time: 115 us
  Pallas kernels  38.1 us (33%)
  blocking collectives  34.6 us (30%)
  waiting for transfers between devices  26.5 us (23%)
  starting transfers between devices  14.6 us (13%)
    all_to_all x1, blocking collectives, per_device(): lax.all_to_all(power, ('gx', 'gy'), split_axis=0, concat_axis=0, tiled=True)  34.6 us
    all_to_all x1, waiting for transfers between devices, per_device(): piece = lax.all_to_all(sent, 'gx', split_axis=0, concat_axis=0, tiled=True)  26.5 us
    pallas_call x1, Pallas kernels, weights(): pl.pallas_call(functools.partial(weights_kernel, local_chans), grid=(loca...  24.2 us
    all_to_all x1, starting transfers between devices, per_device(): piece = lax.all_to_all(sent, 'gx', split_axis=0, concat_axis=0, tiled=True)  14.6 us
    pallas_call x1, Pallas kernels, form_beams(): pl.pallas_call(beams_kernel, in_specs=[pl.BlockSpec(memory_space=pltpu.HB...  9.13 us
    pallas_call x1, Pallas kernels, regroup(): pl.pallas_call(regroup_kernel, in_specs=[pl.BlockSpec(memory_space=pltpu....  2.6 us
  transfers between devices with their start and end apart: 1, of which 1 were waited for; matrix products, arithmetic and copies ran while one was open for 0% of the time, Pallas kernels for 21%

profile of v3, /device:TPU:1, one launch (start us, length us, event | category | flops | bytes accessed | tf_op | source)
XLA Modules:
  0.0 114.6 jit_solution(12997921029591471673)
XLA Ops:
  0.6 2.6 %regroup.1 = bf16[64,2,64,128]{3,2,1,0:T(8,128)(2,1)} custom-call(bf16[2,64,64,128]{3,2,1,0:T(8,128)(2,1)} %v_ref.1), custom_call_target="tpu_custom_call" | custom-call | tf_op jit(solution)/shard_map/regroup/pallas_call | solution.py:63
  3.2 0.0 copy-start.3
  3.2 0.0 copy-start.1
  3.3 0.0 copy-start.2
  3.3 14.6 %all-to-all-start = ((bf16[64,2,64,128]{3,2,1,0:T(8,128)(2,1)}), bf16[64,2,64,128]{3,2,1,0:T(8,128)(2,1)S(1)}, u32[]{:S(2)}, u32[]{:S(2)}) async-start(bf16[64,2,64,128]{3,2,1,0:T(8,128)(2,1)} %regroup.1), calls=%async_computation | async-start | bytes 4194304 | tf_op jit(solution)/shard_map/all_to_all | solution.py:312
  17.9 0.0 copy-done.3
  17.9 0.1 convert_element_type.10
  18.0 0.1 reshape.19.flags_ref
  18.0 0.0 copy-done.1
  18.0 0.0 copy-done.2
  18.1 0.0 copy-start
  18.1 24.2 %weights.1.w_hbm = bf16[2,1024,4096]{2,1,0:T(8,128)(2,1)} custom-call(s32[2,1024]{1,0:T(2,128)S(1)} %bitcast.12, s32[2,2048]{1,0:T(2,128)S(1)} %bitcast.11), custom_call_target="tpu_custom_call" | custom-call | flops 2516582400 | bytes 16777216 | tf_op jit(solution)/shard_map/weights/pallas_call | solution.py:120
  42.2 26.5 %all-to-all-done = bf16[64,2,64,128]{3,2,1,0:T(8,128)(2,1)S(1)} async-done(((bf16[64,2,64,128]{3,2,1,0:T(8,128)(2,1)}), bf16[64,2,64,128]{3,2,1,0:T(8,128)(2,1)S(1)}, u32[]{:S(2)}, u32[]{:S(2)}) %all-to-all-start) | async-done | bytes 2097184 | tf_op jit(solution)/shard_map/all_to_all | solution.py:312
  68.8 0.0 copy-done
  68.8 9.1 %beams.1 = bf16[2048,128]{1,0:T(8,128)(2,1)S(1)} custom-call(bf16[2,1024,4096]{2,1,0:T(8,128)(2,1)} %weights.1.w_hbm, bf16[32,2,2,64,128]{4,3,2,1,0:T(8,128)(2,1)S(1)} %bitcast.8, bf16[512,256]{1,0:T(8,128)(2,1)S(1)} %copy-done, f32[2,128]{1,0:T(2,128)S(1)} %reshape.19.flags_ref), custom_call_target="tpu_custom_call" | custom-call | tf_op jit(solution)/shard_map/beams/pallas_call | solution.py:234
  77.9 34.6 %all_to_all.10 = bf16[512,4,128]{2,1,0:T(4,128)(2,1)S(1)} all-to-all(bf16[512,4,128]{2,1,0:T(4,128)(2,1)S(1)} %bitcast.9), channel_id=1, replica_groups=mesh['gx'=32,'gy'=16] {'gx','gy'}, dimensions={0} | all-to-all | bytes 1048576 | tf_op jit(solution)/shard_map/all_to_all | solution.py:318
  112.5 2.2 %finish.1 = (bf16[2,8,16384]{2,1,0:T(8,128)(2,1)}, f32[2,2,16384]{2,1,0:T(2,128)}) custom-call(bf16[2048,128]{1,0:T(8,128)(2,1)S(1)} %bitcast.10), custom_call_target="tpu_custom_call" | custom-call | tf_op jit(solution)/shard_map/finish/pallas_call | solution.py:296
  (2 shorter events, 0.0 us)
Async XLA Ops:
  3.2 14.6 %copy-start.3 = (s32[8,32]{1,0:T(8,128)S(1)}, s32[8,32]{1,0:T(8,128)}, u32[]{:S(2)}) copy-start(s32[8,32]{1,0:T(8,128)} %param.8) | copy-start | bytes 3076
  3.2 14.8 %copy-start.1 = (s32[2048,2]{0,1:T(2,128)S(1)}, s32[2048,2]{0,1:T(2,128)}, u32[]{:S(2)}) copy-start(s32[2048,2]{0,1:T(2,128)} %param.7) | copy-start | bytes 49156
  3.3 14.8 %copy-start.2 = (s32[1024,2]{0,1:T(2,128)S(1)}, s32[1024,2]{0,1:T(2,128)}, u32[]{:S(2)}) copy-start(s32[1024,2]{0,1:T(2,128)} %param.6) | copy-start | bytes 24580
  3.3 65.5 %all-to-all-start = ((bf16[64,2,64,128]{3,2,1,0:T(8,128)(2,1)}), bf16[64,2,64,128]{3,2,1,0:T(8,128)(2,1)S(1)}, u32[]{:S(2)}, u32[]{:S(2)}) async-start(bf16[64,2,64,128]{3,2,1,0:T(8,128)(2,1)} %regroup.1), calls=%async_computation | async-start | bytes 4194304 | tf_op jit(solution)/shard_map/all_to_all | solution.py:312
  18.1 50.7 %copy-start = (bf16[512,256]{1,0:T(8,128)(2,1)S(1)}, bf16[512,256]{1,0:T(8,128)(2,1)}, u32[]{:S(2)}) copy-start(bf16[512,256]{1,0:T(8,128)(2,1)} %constant.2.clone.table_ref) | copy-start | bytes 786436

commit v4 on v3

--- a/solution.py
+++ b/solution.py
@@ -14,6 +14,7 @@
 UPCHAN = 16
 TOUT = 8
 TIME = 128
+ROWS = 256
 F32 = jnp.float32
 BF16 = jnp.bfloat16
 
@@ -34,7 +35,7 @@
 
 
 def regroup_kernel(v_ref, out_ref, in_buf, out_buf, in_sem, out_sem):
-    parts, feeds, chans, _ = v_ref.shape
+    parts, feeds, chans, time = v_ref.shape
     pieces = [(part, f) for f in range(0, feeds, 16) for part in range(parts)]
 
     def fetch(n):
@@ -42,7 +43,7 @@
         return pltpu.make_async_copy(v_ref.at[at], in_buf.at[at], in_sem.at[n])
 
     def store(n):
-        at = (slice(None), pieces[n][0], pl.ds(pieces[n][1], 16))
+        at = (slice(None), pl.ds(n * 16, 16))
         return pltpu.make_async_copy(out_buf.at[at], out_ref.at[at], out_sem.at[n])
 
     for n in range(len(pieces)):
@@ -50,26 +51,27 @@
     for n, (part, f) in enumerate(pieces):
         fetch(n).wait()
         for c in range(0, chans, 16):
-            tile = in_buf[part, f : f + 16, c : c + 16]
-            out_buf[c : c + 16, part, f : f + 16, :] = jnp.swapaxes(tile, 0, 1)
-        store(n).start()
-    for n in range(len(pieces)):
+            tile = jnp.swapaxes(in_buf[part, f : f + 16, c : c + 16], 0, 1)
+            out_buf[c : c + 16, f : f + 16, part * time : (part + 1) * time] = tile
+        if part == parts - 1:
+            store(f // 16).start()
+    for n in range(feeds // 16):
         store(n).wait()
 
 
 def regroup(v):
     parts, feeds, chans, time = v.shape
-    count = parts * feeds // 16
+    shape = (chans, feeds, parts * time)
     return pl.pallas_call(
         regroup_kernel,
         in_specs=[pl.BlockSpec(memory_space=pltpu.HBM)],
         out_specs=pl.BlockSpec(memory_space=pltpu.HBM),
-        out_shape=pltpu.HBM((chans, parts, feeds, time), BF16),
+        out_shape=pltpu.HBM(shape, BF16),
         scratch_shapes=[
             pltpu.VMEM(v.shape, BF16),
-            pltpu.VMEM((chans, parts, feeds, time), BF16),
-            pltpu.SemaphoreType.DMA((count,)),
-            pltpu.SemaphoreType.DMA((count,)),
+            pltpu.VMEM(shape, BF16),
+            pltpu.SemaphoreType.DMA((parts * feeds // 16,)),
+            pltpu.SemaphoreType.DMA((feeds // 16,)),
         ],
         compiler_params=pltpu.CompilerParams(vmem_limit_bytes=16 * 2**20),
         name="regroup",
@@ -108,8 +110,8 @@
             s = -SIN[-1] * scale
             for coef in SIN[-2::-1]:
                 s = s * u - coef * scale
-            out_ref[0, pl.ds(r0, 16), c0 : c0 + width] = c.astype(BF16)
-            out_ref[0, pl.ds(r0, 16), FEEDS + c0 : FEEDS + c0 + width] = (s * r).astype(BF16)
+            out_ref[0, 0, 0, pl.ds(r0, 16), c0 : c0 + width] = c.astype(BF16)
+            out_ref[0, 0, 1, pl.ds(r0, 16), c0 : c0 + width] = (s * r).astype(BF16)
         return carry
 
     lax.fori_loop(0, bm // 16, chunk, 0)
@@ -117,6 +119,7 @@
 
 def weights(beam_grid, feed_pos, local_chans):
     bm = 128
+    per = ROWS // bm
     return pl.pallas_call(
         functools.partial(weights_kernel, local_chans),
         grid=(local_chans, BEAMS // bm),
@@ -124,8 +127,8 @@
             pl.BlockSpec((2, bm), lambda c, m: (0, m)),
             pl.BlockSpec((2, FEEDS), lambda c, m: (0, 0)),
         ],
-        out_specs=pl.BlockSpec((1, bm, 2 * FEEDS), lambda c, m: (c, m, 0)),
-        out_shape=pltpu.HBM((local_chans, BEAMS, 2 * FEEDS), BF16),
+        out_specs=pl.BlockSpec((1, 1, 2, bm, FEEDS), lambda c, m: (c, m // per, 0, m % per, 0)),
+        out_shape=pltpu.HBM((local_chans, BEAMS // ROWS, 2, ROWS, FEEDS), BF16),
         scratch_shapes=[pltpu.VMEM((bm, FEEDS), F32)],
         compiler_params=pltpu.CompilerParams(vmem_limit_bytes=24 * 2**20),
         cost_estimate=pl.CostEstimate(
@@ -143,26 +146,19 @@
 
 
 def beams_kernel(
-    w_hbm, v_ref, table_ref, flags_ref, out_ref, w_buf, sem, rhs_ref, beam_ref, inten_ref, rows_ref, sum_ref
+    w_hbm, v_ref, table_ref, flags_ref, out_ref, w_buf, sem, beam_ref, inten_ref, sum_ref, rows_ref
 ):
-    slots, bm, _ = w_buf.shape
-    steps = BEAMS // bm
+    slots = w_buf.shape[0]
+    steps = BEAMS // ROWS
     size = 2 * TIME
 
     def fetch(i):
-        rows = pl.ds(pl.multiple_of(i % steps * bm, bm), bm)
-        return pltpu.make_async_copy(w_hbm.at[i // steps, rows], w_buf.at[i % slots], sem.at[i % slots])
+        return pltpu.make_async_copy(w_hbm.at[i // steps, i % steps], w_buf.at[i % slots], sem.at[i % slots])
 
     for i in range(slots):
         fetch(i).start()
-    for chan in range(2):
-        real = v_ref[:, chan, 0].reshape(FEEDS, TIME)
-        imag = v_ref[:, chan, 1].reshape(FEEDS, TIME)
-        rhs_ref[chan, :FEEDS, :TIME] = real
-        rhs_ref[chan, :FEEDS, TIME:] = imag
-        rhs_ref[chan, FEEDS:, :TIME] = -imag
-        rhs_ref[chan, FEEDS:, TIME:] = real
     beam_ref[1] = jnp.zeros_like(beam_ref[1])
+    sum_ref[...] = jnp.zeros_like(sum_ref)
 
     def detect(i):
         high, low = split(beam_ref[i % 2])
@@ -172,10 +168,9 @@
             + jnp.dot(low, table_ref[:size], preferred_element_type=F32)
         )
         real, imag = fine[:, :TIME], fine[:, TIME:]
-        rows = pl.ds(pl.multiple_of(i % steps * bm, bm), bm)
-        x = real * real + imag * imag
-        inten_ref[i // steps, rows, :] = x
-        sum_ref[i] = jnp.sum(x.reshape(bm // 8, 8, TIME), axis=0)
+        intensity = real * real + imag * imag
+        inten_ref[pl.ds(pl.multiple_of(i * ROWS, ROWS), ROWS), :] = intensity
+        sum_ref[i] = jnp.sum(intensity.reshape(ROWS // 8, 8, TIME), axis=0)
 
     def normalize(chan):
         total = jnp.sum(sum_ref[chan * steps : (chan + 1) * steps], axis=0)
@@ -187,7 +182,7 @@
 
         def move(j, carry):
             for beam in range(2):
-                x = inten_ref[chan, pl.ds(j * 128 + beam, 64, stride=2), :]
+                x = inten_ref[pl.ds(chan * BEAMS + j * 128 + beam, 64, stride=2), :]
                 rows_ref[pl.ds(j * 256 + 2 * chan + beam, 64, stride=4), :] = x * scale
             if chan == 1:
                 rows = pl.ds(pl.multiple_of(j * 256, 256), 256)
@@ -198,9 +193,11 @@
 
     def body(i, carry):
         fetch(i).wait()
-        beam = jnp.dot(w_buf[i % slots], rhs_ref[i // steps], preferred_element_type=F32)
+        rhs = v_ref[:, i // steps].reshape(FEEDS, size)
+        part = jnp.dot(w_buf[i % slots].reshape(2 * ROWS, FEEDS), rhs, preferred_element_type=F32)
         detect(jnp.maximum(i - 1, 0))
-        beam_ref[i % 2] = beam
+        beam_ref[i % 2, :, :TIME] = part[:ROWS, :TIME] - part[ROWS:, TIME:]
+        beam_ref[i % 2, :, TIME:] = part[:ROWS, TIME:] + part[ROWS:, :TIME]
 
         @pl.when(i + slots < 2 * steps)
         def _():
@@ -229,7 +226,7 @@
 
 
 def form_beams(w, v, flags):
-    bm, slots = 256, 4
+    slots = 4
     vmem = pl.BlockSpec(memory_space=pltpu.VMEM)
     return pl.pallas_call(
         beams_kernel,
@@ -237,13 +234,12 @@
         out_specs=vmem,
         out_shape=jax.ShapeDtypeStruct((2 * BEAMS, TIME), BF16),
         scratch_shapes=[
-            pltpu.VMEM((slots, bm, 2 * FEEDS), BF16),
+            pltpu.VMEM((slots, 2, ROWS, FEEDS), BF16),
             pltpu.SemaphoreType.DMA((slots,)),
-            pltpu.VMEM((2, 2 * FEEDS, 2 * TIME), BF16),
-            pltpu.VMEM((2, bm, 2 * TIME), F32),
-            pltpu.VMEM((2, BEAMS, TIME), F32),
+            pltpu.VMEM((2, ROWS, 2 * TIME), F32),
             pltpu.VMEM((2 * BEAMS, TIME), F32),
-            pltpu.VMEM((2 * BEAMS // bm, 8, TIME), F32),
+            pltpu.VMEM((2 * BEAMS // ROWS, 8, TIME), F32),
+            pltpu.VMEM((2 * BEAMS, TIME), F32),
         ],
         compiler_params=pltpu.CompilerParams(vmem_limit_bytes=32 * 2**20),
         name="beams",
@@ -272,6 +268,11 @@
                 for i in range(8):
                     if i & bit == 0:
                         low, high = tiles[i], tiles[i | bit]
+                        if bit == 4:
+                            moved = pltpu.roll(jnp.where(upper, low, high), 64, 1)
+                            tiles[i] = jnp.where(upper, moved, low)
+                            tiles[i | bit] = jnp.where(upper, high, moved)
+                            continue
                         tiles[i] = jnp.where(upper, pltpu.roll(high, 16 * bit, 1), low)
                         tiles[i | bit] = jnp.where(upper, high, pltpu.roll(low, TIME - 16 * bit, 1))
             total = sum(tiles[1:], tiles[0])
@@ -312,7 +313,7 @@
     piece = lax.all_to_all(sent, "gx", split_axis=0, concat_axis=0, tiled=True)
     w = weights(beam_grid, feed_pos, local_chans)
     flags = rfi_mask.reshape(TOUT, local_chans, UPCHAN).transpose(1, 0, 2).astype(F32)
-    piece = piece.reshape(inputs, local_chans, 2, voltages.shape[1], TIME)
+    piece = piece.reshape(inputs, local_chans, voltages.shape[1], 2 * TIME)
     power = form_beams(w, piece, flags.reshape(local_chans, TIME))
     power = power.reshape(512, 4, TIME)
     power = lax.all_to_all(power, ("gx", "gy"), split_axis=0, concat_axis=0, tiled=True)

time: 115 us -> 115 us (level)
  no operation moved by 1% of the time
where the time goes in v4:
time: 115 us
  Pallas kernels  38.4 us (33%)
  blocking collectives  34.6 us (30%)
  waiting for transfers between devices  26.2 us (23%)
  starting transfers between devices  14.6 us (13%)
    all_to_all x1, blocking collectives, per_device(): lax.all_to_all(power, ('gx', 'gy'), split_axis=0, concat_axis=0, tiled=True)  34.6 us
    all_to_all x1, waiting for transfers between devices, per_device(): piece = lax.all_to_all(sent, 'gx', split_axis=0, concat_axis=0, tiled=True)  26.2 us
    pallas_call x1, Pallas kernels, weights(): pl.pallas_call(functools.partial(weights_kernel, local_chans), grid=(loca...  24.5 us
    all_to_all x1, starting transfers between devices, per_device(): piece = lax.all_to_all(sent, 'gx', split_axis=0, concat_axis=0, tiled=True)  14.6 us
    pallas_call x1, Pallas kernels, form_beams(): pl.pallas_call(beams_kernel, in_specs=[pl.BlockSpec(memory_space=pltpu.HB...  9.1 us
    pallas_call x1, Pallas kernels, regroup(): pl.pallas_call(regroup_kernel, in_specs=[pl.BlockSpec(memory_space=pltpu....  2.61 us
  transfers between devices with their start and end apart: 1, of which 1 were waited for; matrix products, arithmetic and copies ran while one was open for 0% of the time, Pallas kernels for 21%

profile of v4, /device:TPU:1, one launch (start us, length us, event | category | flops | bytes accessed | tf_op | source)
XLA Modules:
  0.0 114.6 jit_solution(14026349201807941949)
XLA Ops:
  0.6 2.6 %regroup.1 = bf16[64,64,256]{2,1,0:T(8,128)(2,1)} custom-call(bf16[2,64,64,128]{3,2,1,0:T(8,128)(2,1)} %v_ref.1), custom_call_target="tpu_custom_call" | custom-call | tf_op jit(solution)/shard_map/regroup/pallas_call | solution.py:65
  3.2 0.0 copy-start.3
  3.3 0.0 copy-start.1
  3.3 0.0 copy-start.2
  3.3 14.6 %all-to-all-start = ((bf16[64,64,256]{2,1,0:T(8,128)(2,1)}), bf16[64,64,256]{2,1,0:T(8,128)(2,1)S(1)}, u32[]{:S(2)}, u32[]{:S(2)}) async-start(bf16[64,64,256]{2,1,0:T(8,128)(2,1)} %regroup.1), calls=%async_computation | async-start | bytes 4194304 | tf_op jit(solution)/shard_map/all_to_all | solution.py:313
  17.9 0.0 copy-done.3
  17.9 0.1 convert_element_type.10
  18.0 0.1 reshape.19.flags_ref
  18.1 0.0 copy-done.1
  18.1 0.0 copy-done.2
  18.1 0.0 copy-start
  18.1 24.5 %weights.1.w_hbm = bf16[2,4,2,256,2048]{4,3,2,1,0:T(8,128)(2,1)} custom-call(s32[2,1024]{1,0:T(2,128)S(1)} %bitcast.12, s32[2,2048]{1,0:T(2,128)S(1)} %bitcast.11), custom_call_target="tpu_custom_call" | custom-call | flops 2516582400 | bytes 16777216 | tf_op jit(solution)/shard_map/weights/pallas_call | solution.py:123
  42.5 26.2 %all-to-all-done = bf16[64,64,256]{2,1,0:T(8,128)(2,1)S(1)} async-done(((bf16[64,64,256]{2,1,0:T(8,128)(2,1)}), bf16[64,64,256]{2,1,0:T(8,128)(2,1)S(1)}, u32[]{:S(2)}, u32[]{:S(2)}) %all-to-all-start) | async-done | bytes 2097184 | tf_op jit(solution)/shard_map/all_to_all | solution.py:313
  68.8 0.0 copy-done
  68.8 9.1 %beams.1 = bf16[2048,128]{1,0:T(8,128)(2,1)S(1)} custom-call(bf16[2,4,2,256,2048]{4,3,2,1,0:T(8,128)(2,1)} %weights.1.w_hbm, bf16[32,2,64,256]{3,2,1,0:T(8,128)(2,1)S(1)} %bitcast.8, bf16[512,256]{1,0:T(8,128)(2,1)S(1)} %copy-done, f32[2,128]{1,0:T(2,128)S(1)} %reshape.19.flags_ref), custom_call_target="tpu_custom_call" | custom-call | tf_op jit(solution)/shard_map/beams/pallas_call | solution.py:231
  77.9 34.6 %all_to_all.10 = bf16[512,4,128]{2,1,0:T(4,128)(2,1)S(1)} all-to-all(bf16[512,4,128]{2,1,0:T(4,128)(2,1)S(1)} %bitcast.9), channel_id=1, replica_groups=mesh['gx'=32,'gy'=16] {'gx','gy'}, dimensions={0} | all-to-all | bytes 1048576 | tf_op jit(solution)/shard_map/all_to_all | solution.py:319
  112.4 2.2 %finish.1 = (bf16[2,8,16384]{2,1,0:T(8,128)(2,1)}, f32[2,2,16384]{2,1,0:T(2,128)}) custom-call(bf16[2048,128]{1,0:T(8,128)(2,1)S(1)} %bitcast.10), custom_call_target="tpu_custom_call" | custom-call | tf_op jit(solution)/shard_map/finish/pallas_call | solution.py:297
  (2 shorter events, 0.0 us)
Async XLA Ops:
  3.2 14.6 %copy-start.3 = (s32[8,32]{1,0:T(8,128)S(1)}, s32[8,32]{1,0:T(8,128)}, u32[]{:S(2)}) copy-start(s32[8,32]{1,0:T(8,128)} %param.8) | copy-start | bytes 3076
  3.3 14.8 %copy-start.1 = (s32[2048,2]{0,1:T(2,128)S(1)}, s32[2048,2]{0,1:T(2,128)}, u32[]{:S(2)}) copy-start(s32[2048,2]{0,1:T(2,128)} %param.7) | copy-start | bytes 49156
  3.3 14.8 %copy-start.2 = (s32[1024,2]{0,1:T(2,128)S(1)}, s32[1024,2]{0,1:T(2,128)}, u32[]{:S(2)}) copy-start(s32[1024,2]{0,1:T(2,128)} %param.6) | copy-start | bytes 24580
  3.3 65.5 %all-to-all-start = ((bf16[64,64,256]{2,1,0:T(8,128)(2,1)}), bf16[64,64,256]{2,1,0:T(8,128)(2,1)S(1)}, u32[]{:S(2)}, u32[]{:S(2)}) async-start(bf16[64,64,256]{2,1,0:T(8,128)(2,1)} %regroup.1), calls=%async_computation | async-start | bytes 4194304 | tf_op jit(solution)/shard_map/all_to_all | solution.py:313
  18.1 50.7 %copy-start = (bf16[512,256]{1,0:T(8,128)(2,1)S(1)}, bf16[512,256]{1,0:T(8,128)(2,1)}, u32[]{:S(2)}) copy-start(bf16[512,256]{1,0:T(8,128)(2,1)} %constant.2.clone.table_ref) | copy-start | bytes 786436

commit v5 on v3

--- a/solution.py
+++ b/solution.py
@@ -76,7 +76,7 @@
     )(pltpu.with_memory_space_constraint(v, pltpu.HBM))
 
 
-def weights_kernel(local_chans, beam_ref, feed_ref, out_ref, turns_ref):
+def weights_kernel(local_chans, beam_ref, feed_ref, out_ref, head_ref, turns_ref):
     device = lax.axis_index("gy") * lax.axis_size("gx") + lax.axis_index("gx")
     factor = (device * local_chans + pl.program_id(0) + 400) % 4096
     bm = beam_ref.shape[1]
@@ -114,6 +114,10 @@
 
     lax.fori_loop(0, bm // 16, chunk, 0)
 
+    @pl.when((pl.program_id(0) == 0) & (pl.program_id(1) == 0))
+    def _():
+        head_ref[...] = out_ref[0]
+
 
 def weights(beam_grid, feed_pos, local_chans):
     bm = 128
@@ -124,8 +128,14 @@
             pl.BlockSpec((2, bm), lambda c, m: (0, m)),
             pl.BlockSpec((2, FEEDS), lambda c, m: (0, 0)),
         ],
-        out_specs=pl.BlockSpec((1, bm, 2 * FEEDS), lambda c, m: (c, m, 0)),
-        out_shape=pltpu.HBM((local_chans, BEAMS, 2 * FEEDS), BF16),
+        out_specs=(
+            pl.BlockSpec((1, bm, 2 * FEEDS), lambda c, m: (c, m, 0)),
+            pl.BlockSpec((bm, 2 * FEEDS), lambda c, m: (0, 0)),
+        ),
+        out_shape=(
+            pltpu.HBM((local_chans, BEAMS, 2 * FEEDS), BF16),
+            jax.ShapeDtypeStruct((bm, 2 * FEEDS), BF16),
+        ),
         scratch_shapes=[pltpu.VMEM((bm, FEEDS), F32)],
         compiler_params=pltpu.CompilerParams(vmem_limit_bytes=24 * 2**20),
         cost_estimate=pl.CostEstimate(
@@ -143,7 +153,7 @@
 
 
 def beams_kernel(
-    w_hbm, v_ref, table_ref, flags_ref, out_ref, w_buf, sem, rhs_ref, beam_ref, inten_ref, rows_ref, sum_ref
+    w_hbm, head_ref, v_ref, table_ref, flags_ref, out_ref, w_buf, sem, rhs_ref, beam_ref, inten_ref, rows_ref, sum_ref
 ):
     slots, bm, _ = w_buf.shape
     steps = BEAMS // bm
@@ -153,7 +163,11 @@
         rows = pl.ds(pl.multiple_of(i % steps * bm, bm), bm)
         return pltpu.make_async_copy(w_hbm.at[i // steps, rows], w_buf.at[i % slots], sem.at[i % slots])
 
-    for i in range(slots):
+    kept = head_ref.shape[0]
+    rest = pl.ds(kept, bm - kept)
+    pltpu.make_async_copy(w_hbm.at[0, rest], w_buf.at[0, rest], sem.at[0]).start()
+    pltpu.make_async_copy(head_ref, w_buf.at[0, pl.ds(0, kept)], sem.at[0]).start()
+    for i in range(1, slots):
         fetch(i).start()
     for chan in range(2):
         real = v_ref[:, chan, 0].reshape(FEEDS, TIME)
@@ -228,12 +242,12 @@
     return np.concatenate([high, low], 0)
 
 
-def form_beams(w, v, flags):
+def form_beams(w, head, v, flags):
     bm, slots = 256, 4
     vmem = pl.BlockSpec(memory_space=pltpu.VMEM)
     return pl.pallas_call(
         beams_kernel,
-        in_specs=[pl.BlockSpec(memory_space=pltpu.HBM), vmem, vmem, vmem],
+        in_specs=[pl.BlockSpec(memory_space=pltpu.HBM), vmem, vmem, vmem, vmem],
         out_specs=vmem,
         out_shape=jax.ShapeDtypeStruct((2 * BEAMS, TIME), BF16),
         scratch_shapes=[
@@ -247,7 +261,7 @@
         ],
         compiler_params=pltpu.CompilerParams(vmem_limit_bytes=32 * 2**20),
         name="beams",
-    )(pltpu.with_memory_space_constraint(w, pltpu.HBM), v, jnp.asarray(dft_table()), flags)
+    )(pltpu.with_memory_space_constraint(w, pltpu.HBM), head, v, jnp.asarray(dft_table()), flags)
 
 
 def finish_kernel(in_ref, power_ref, sums_ref):
@@ -310,10 +324,10 @@
     local_chans = chan_dev // inputs
     sent = regroup(voltages)
     piece = lax.all_to_all(sent, "gx", split_axis=0, concat_axis=0, tiled=True)
-    w = weights(beam_grid, feed_pos, local_chans)
+    w, head = weights(beam_grid, feed_pos, local_chans)
     flags = rfi_mask.reshape(TOUT, local_chans, UPCHAN).transpose(1, 0, 2).astype(F32)
     piece = piece.reshape(inputs, local_chans, 2, voltages.shape[1], TIME)
-    power = form_beams(w, piece, flags.reshape(local_chans, TIME))
+    power = form_beams(w, head, piece, flags.reshape(local_chans, TIME))
     power = power.reshape(512, 4, TIME)
     power = lax.all_to_all(power, ("gx", "gy"), split_axis=0, concat_axis=0, tiled=True)
     return finish(power.reshape(2048, TIME))

time: 115 us -> 115 us (level)
  no operation moved by 1% of the time
where the time goes in v5:
time: 115 us; the launch traced here: 114 us
  Pallas kernels  37.9 us (33%)
  blocking collectives  34.6 us (30%)
  waiting for transfers between devices  26.3 us (23%)
  starting transfers between devices  14.6 us (13%)
    all_to_all x1, blocking collectives, per_device(): lax.all_to_all(power, ('gx', 'gy'), split_axis=0, concat_axis=0, tiled=True)  34.6 us
    all_to_all x1, waiting for transfers between devices, per_device(): piece = lax.all_to_all(sent, 'gx', split_axis=0, concat_axis=0, tiled=True)  26.3 us
    pallas_call x1, Pallas kernels, weights(): pl.pallas_call(functools.partial(weights_kernel, local_chans), grid=(loca...  24.4 us
    all_to_all x1, starting transfers between devices, per_device(): piece = lax.all_to_all(sent, 'gx', split_axis=0, concat_axis=0, tiled=True)  14.6 us
    pallas_call x1, Pallas kernels, form_beams(): pl.pallas_call(beams_kernel, in_specs=[pl.BlockSpec(memory_space=pltpu.HB...  8.76 us
    pallas_call x1, Pallas kernels, regroup(): pl.pallas_call(regroup_kernel, in_specs=[pl.BlockSpec(memory_space=pltpu....  2.64 us
  transfers between devices with their start and end apart: 1, of which 1 were waited for; matrix products, arithmetic and copies ran while one was open for 0% of the time, Pallas kernels for 21%

profile of v5, /device:TPU:1, one launch (start us, length us, event | category | flops | bytes accessed | tf_op | source)
XLA Modules:
  0.0 114.3 jit_solution(5941964054335665678)
XLA Ops:
  0.6 2.6 %regroup.1 = bf16[64,2,64,128]{3,2,1,0:T(8,128)(2,1)} custom-call(bf16[2,64,64,128]{3,2,1,0:T(8,128)(2,1)} %v_ref.1), custom_call_target="tpu_custom_call" | custom-call | tf_op jit(solution)/shard_map/regroup/pallas_call | solution.py:63
  3.3 0.0 copy-start.3
  3.3 0.0 copy-start.1
  3.3 0.0 copy-start.2
  3.3 14.6 %all-to-all-start = ((bf16[64,2,64,128]{3,2,1,0:T(8,128)(2,1)}), bf16[64,2,64,128]{3,2,1,0:T(8,128)(2,1)S(1)}, u32[]{:S(2)}, u32[]{:S(2)}) async-start(bf16[64,2,64,128]{3,2,1,0:T(8,128)(2,1)} %regroup.1), calls=%async_computation | async-start | bytes 4194304 | tf_op jit(solution)/shard_map/all_to_all | solution.py:326
  17.9 0.0 copy-done.3
  17.9 0.1 convert_element_type.10
  18.0 0.1 reshape.19.flags_ref
  18.1 0.0 copy-done.1
  18.1 0.0 copy-done.2
  18.1 0.0 copy-start
  18.1 24.4 %weights.1 = (bf16[2,1024,4096]{2,1,0:T(8,128)(2,1)}, bf16[128,4096]{1,0:T(8,128)(2,1)S(1)}) custom-call(s32[2,1024]{1,0:T(2,128)S(1)} %bitcast.12, s32[2,2048]{1,0:T(2,128)S(1)} %bitcast.11), custom_call_target="tpu_custom_call" | custom-call | flops 2516582400 | bytes 16777216 | tf_op jit(solution)/shard_map/weights/pallas_call | solution.py:124
  42.5 26.3 %all-to-all-done = bf16[64,2,64,128]{3,2,1,0:T(8,128)(2,1)S(1)} async-done(((bf16[64,2,64,128]{3,2,1,0:T(8,128)(2,1)}), bf16[64,2,64,128]{3,2,1,0:T(8,128)(2,1)S(1)}, u32[]{:S(2)}, u32[]{:S(2)}) %all-to-all-start) | async-done | bytes 2097184 | tf_op jit(solution)/shard_map/all_to_all | solution.py:326
  68.8 0.0 copy-done
  68.8 8.8 %beams.1 = bf16[2048,128]{1,0:T(8,128)(2,1)S(1)} custom-call(bf16[2,1024,4096]{2,1,0:T(8,128)(2,1)} %get-tuple-element.4.w_hbm, bf16[128,4096]{1,0:T(8,128)(2,1)S(1)} %get-tuple-element.5.head_ref, bf16[32,2,2,64,128]{4,3,2,1,0:T(8,128)(2,1)S(1)} %bitcast.8, bf16[512,256]{1,0:T(8,128)(2,1)S(1)} %copy-done, f32[2,128]{1,0:T(2,128)S(1)} %reshape.19.flags_ref), custom_call_target="tpu_custom_call" | custom-call | tf_op jit(solution)/shard_map/beams/pallas_call | solution.py:248
  77.6 34.6 %all_to_all.10 = bf16[512,4,128]{2,1,0:T(4,128)(2,1)S(1)} all-to-all(bf16[512,4,128]{2,1,0:T(4,128)(2,1)S(1)} %bitcast.10), channel_id=1, replica_groups=mesh['gx'=32,'gy'=16] {'gx','gy'}, dimensions={0} | all-to-all | bytes 1048576 | tf_op jit(solution)/shard_map/all_to_all | solution.py:332
  112.1 2.2 %finish.1 = (bf16[2,8,16384]{2,1,0:T(8,128)(2,1)}, f32[2,2,16384]{2,1,0:T(2,128)}) custom-call(bf16[2048,128]{1,0:T(8,128)(2,1)S(1)} %bitcast.9), custom_call_target="tpu_custom_call" | custom-call | tf_op jit(solution)/shard_map/finish/pallas_call | solution.py:310
  (2 shorter events, 0.0 us)
Async XLA Ops:
  3.3 14.6 %copy-start.3 = (s32[8,32]{1,0:T(8,128)S(1)}, s32[8,32]{1,0:T(8,128)}, u32[]{:S(2)}) copy-start(s32[8,32]{1,0:T(8,128)} %param.8) | copy-start | bytes 3076
  3.3 14.8 %copy-start.1 = (s32[2048,2]{0,1:T(2,128)S(1)}, s32[2048,2]{0,1:T(2,128)}, u32[]{:S(2)}) copy-start(s32[2048,2]{0,1:T(2,128)} %param.7) | copy-start | bytes 49156
  3.3 14.8 %copy-start.2 = (s32[1024,2]{0,1:T(2,128)S(1)}, s32[1024,2]{0,1:T(2,128)}, u32[]{:S(2)}) copy-start(s32[1024,2]{0,1:T(2,128)} %param.6) | copy-start | bytes 24580
  3.3 65.5 %all-to-all-start = ((bf16[64,2,64,128]{3,2,1,0:T(8,128)(2,1)}), bf16[64,2,64,128]{3,2,1,0:T(8,128)(2,1)S(1)}, u32[]{:S(2)}, u32[]{:S(2)}) async-start(bf16[64,2,64,128]{3,2,1,0:T(8,128)(2,1)} %regroup.1), calls=%async_computation | async-start | bytes 4194304 | tf_op jit(solution)/shard_map/all_to_all | solution.py:326
  18.1 50.7 %copy-start = (bf16[512,256]{1,0:T(8,128)(2,1)S(1)}, bf16[512,256]{1,0:T(8,128)(2,1)}, u32[]{:S(2)}) copy-start(bf16[512,256]{1,0:T(8,128)(2,1)} %constant.2.clone.table_ref) | copy-start | bytes 786436

commit v6 on v4

--- a/solution.py
+++ b/solution.py
@@ -78,7 +78,7 @@
     )(pltpu.with_memory_space_constraint(v, pltpu.HBM))
 
 
-def weights_kernel(local_chans, beam_ref, feed_ref, out_ref, turns_ref):
+def weights_kernel(local_chans, beam_ref, feed_ref, out_ref, head_ref, turns_ref):
     device = lax.axis_index("gy") * lax.axis_size("gx") + lax.axis_index("gx")
     factor = (device * local_chans + pl.program_id(0) + 400) % 4096
     bm = beam_ref.shape[1]
@@ -116,6 +116,10 @@
 
     lax.fori_loop(0, bm // 16, chunk, 0)
 
+    @pl.when((pl.program_id(0) == 0) & (pl.program_id(1) == 0))
+    def _():
+        head_ref[...] = out_ref[0, 0]
+
 
 def weights(beam_grid, feed_pos, local_chans):
     bm = 128
@@ -127,8 +131,14 @@
             pl.BlockSpec((2, bm), lambda c, m: (0, m)),
             pl.BlockSpec((2, FEEDS), lambda c, m: (0, 0)),
         ],
-        out_specs=pl.BlockSpec((1, 1, 2, bm, FEEDS), lambda c, m: (c, m // per, 0, m % per, 0)),
-        out_shape=pltpu.HBM((local_chans, BEAMS // ROWS, 2, ROWS, FEEDS), BF16),
+        out_specs=(
+            pl.BlockSpec((1, 1, 2, bm, FEEDS), lambda c, m: (c, m // per, 0, m % per, 0)),
+            pl.BlockSpec((2, bm, FEEDS), lambda c, m: (0, 0, 0)),
+        ),
+        out_shape=(
+            pltpu.HBM((local_chans, BEAMS // ROWS, 2, ROWS, FEEDS), BF16),
+            jax.ShapeDtypeStruct((2, bm, FEEDS), BF16),
+        ),
         scratch_shapes=[pltpu.VMEM((bm, FEEDS), F32)],
         compiler_params=pltpu.CompilerParams(vmem_limit_bytes=24 * 2**20),
         cost_estimate=pl.CostEstimate(
@@ -146,7 +156,7 @@
 
 
 def beams_kernel(
-    w_hbm, v_ref, table_ref, flags_ref, out_ref, w_buf, sem, beam_ref, inten_ref, sum_ref, rows_ref
+    w_hbm, head_ref, v_ref, table_ref, flags_ref, out_ref, w_buf, sem, beam_ref, inten_ref, sum_ref, rows_ref
 ):
     slots = w_buf.shape[0]
     steps = BEAMS // ROWS
@@ -155,7 +165,13 @@
     def fetch(i):
         return pltpu.make_async_copy(w_hbm.at[i // steps, i % steps], w_buf.at[i % slots], sem.at[i % slots])
 
-    for i in range(slots):
+    kept = head_ref.shape[1]
+    for part in range(2):
+        rest = pl.ds(kept, ROWS - kept)
+        pltpu.make_async_copy(w_hbm.at[0, 0, part, rest], w_buf.at[0, part, rest], sem.at[0]).start()
+        first = w_buf.at[0, part, pl.ds(0, kept)]
+        pltpu.make_async_copy(head_ref.at[part], first, sem.at[0]).start()
+    for i in range(1, slots):
         fetch(i).start()
     beam_ref[1] = jnp.zeros_like(beam_ref[1])
     sum_ref[...] = jnp.zeros_like(sum_ref)
@@ -225,12 +241,12 @@
     return np.concatenate([high, low], 0)
 
 
-def form_beams(w, v, flags):
+def form_beams(w, head, v, flags):
     slots = 4
     vmem = pl.BlockSpec(memory_space=pltpu.VMEM)
     return pl.pallas_call(
         beams_kernel,
-        in_specs=[pl.BlockSpec(memory_space=pltpu.HBM), vmem, vmem, vmem],
+        in_specs=[pl.BlockSpec(memory_space=pltpu.HBM), vmem, vmem, vmem, vmem],
         out_specs=vmem,
         out_shape=jax.ShapeDtypeStruct((2 * BEAMS, TIME), BF16),
         scratch_shapes=[
@@ -243,7 +259,7 @@
         ],
         compiler_params=pltpu.CompilerParams(vmem_limit_bytes=32 * 2**20),
         name="beams",
-    )(pltpu.with_memory_space_constraint(w, pltpu.HBM), v, jnp.asarray(dft_table()), flags)
+    )(pltpu.with_memory_space_constraint(w, pltpu.HBM), head, v, jnp.asarray(dft_table()), flags)
 
 
 def finish_kernel(in_ref, power_ref, sums_ref):
@@ -311,10 +327,10 @@
     local_chans = chan_dev // inputs
     sent = regroup(voltages)
     piece = lax.all_to_all(sent, "gx", split_axis=0, concat_axis=0, tiled=True)
-    w = weights(beam_grid, feed_pos, local_chans)
+    w, head = weights(beam_grid, feed_pos, local_chans)
     flags = rfi_mask.reshape(TOUT, local_chans, UPCHAN).transpose(1, 0, 2).astype(F32)
     piece = piece.reshape(inputs, local_chans, voltages.shape[1], 2 * TIME)
-    power = form_beams(w, piece, flags.reshape(local_chans, TIME))
+    power = form_beams(w, head, piece, flags.reshape(local_chans, TIME))
     power = power.reshape(512, 4, TIME)
     power = lax.all_to_all(power, ("gx", "gy"), split_axis=0, concat_axis=0, tiled=True)
     return finish(power.reshape(2048, TIME))

time: 115 us -> 115 us (level)
  transfers between devices with their start and end apart: 1 -> 1, of which waited for: 1 -> 1; matrix products, arithmetic and copies ran while one was open for 0% -> 0% of each run, Pallas kernels for 21% -> 22%
where the time goes in v6:
time: 115 us; the launch traced here: 114 us
  Pallas kernels  38.2 us (33%)
  blocking collectives  34.6 us (30%)
  waiting for transfers between devices  26 us (23%)
  starting transfers between devices  14.6 us (13%)
    all_to_all x1, blocking collectives, per_device(): lax.all_to_all(power, ('gx', 'gy'), split_axis=0, concat_axis=0, tiled=True)  34.6 us
    all_to_all x1, waiting for transfers between devices, per_device(): piece = lax.all_to_all(sent, 'gx', split_axis=0, concat_axis=0, tiled=True)  26 us
    pallas_call x1, Pallas kernels, weights(): pl.pallas_call(functools.partial(weights_kernel, local_chans), grid=(loca...  24.7 us
    all_to_all x1, starting transfers between devices, per_device(): piece = lax.all_to_all(sent, 'gx', split_axis=0, concat_axis=0, tiled=True)  14.6 us
    pallas_call x1, Pallas kernels, form_beams(): pl.pallas_call(beams_kernel, in_specs=[pl.BlockSpec(memory_space=pltpu.HB...  8.71 us
    pallas_call x1, Pallas kernels, regroup(): pl.pallas_call(regroup_kernel, in_specs=[pl.BlockSpec(memory_space=pltpu....  2.61 us
  transfers between devices with their start and end apart: 1, of which 1 were waited for; matrix products, arithmetic and copies ran while one was open for 0% of the time, Pallas kernels for 22%

profile of v6, /device:TPU:1, one launch (start us, length us, event | category | flops | bytes accessed | tf_op | source)
XLA Modules:
  0.0 114.3 jit_solution(12944158239418656385)
XLA Ops:
  0.6 2.6 %regroup.1 = bf16[64,64,256]{2,1,0:T(8,128)(2,1)} custom-call(bf16[2,64,64,128]{3,2,1,0:T(8,128)(2,1)} %v_ref.1), custom_call_target="tpu_custom_call" | custom-call | tf_op jit(solution)/shard_map/regroup/pallas_call | solution.py:65
  3.2 0.0 copy-start.3
  3.3 0.0 copy-start.1
  3.3 0.0 copy-start.2
  3.3 14.6 %all-to-all-start = ((bf16[64,64,256]{2,1,0:T(8,128)(2,1)}), bf16[64,64,256]{2,1,0:T(8,128)(2,1)S(1)}, u32[]{:S(2)}, u32[]{:S(2)}) async-start(bf16[64,64,256]{2,1,0:T(8,128)(2,1)} %regroup.1), calls=%async_computation | async-start | bytes 4194304 | tf_op jit(solution)/shard_map/all_to_all | solution.py:329
  17.9 0.0 copy-done.3
  17.9 0.1 convert_element_type.10
  18.0 0.1 reshape.19.flags_ref
  18.1 0.0 copy-done.1
  18.1 0.0 copy-done.2
  18.1 0.0 copy-start
  18.1 24.7 %weights.1 = (bf16[2,4,2,256,2048]{4,3,2,1,0:T(8,128)(2,1)}, bf16[2,128,2048]{2,1,0:T(8,128)(2,1)S(1)}) custom-call(s32[2,1024]{1,0:T(2,128)S(1)} %bitcast.12, s32[2,2048]{1,0:T(2,128)S(1)} %bitcast.11), custom_call_target="tpu_custom_call" | custom-call | flops 2516582400 | bytes 16777216 | tf_op jit(solution)/shard_map/weights/pallas_call | solution.py:127
  42.7 26.0 %all-to-all-done = bf16[64,64,256]{2,1,0:T(8,128)(2,1)S(1)} async-done(((bf16[64,64,256]{2,1,0:T(8,128)(2,1)}), bf16[64,64,256]{2,1,0:T(8,128)(2,1)S(1)}, u32[]{:S(2)}, u32[]{:S(2)}) %all-to-all-start) | async-done | bytes 2097184 | tf_op jit(solution)/shard_map/all_to_all | solution.py:329
  68.8 0.0 copy-done
  68.8 8.7 %beams.1 = bf16[2048,128]{1,0:T(8,128)(2,1)S(1)} custom-call(bf16[2,4,2,256,2048]{4,3,2,1,0:T(8,128)(2,1)} %get-tuple-element.4.w_hbm, bf16[2,128,2048]{2,1,0:T(8,128)(2,1)S(1)} %get-tuple-element.5.head_ref, bf16[32,2,64,256]{3,2,1,0:T(8,128)(2,1)S(1)} %bitcast.8, bf16[512,256]{1,0:T(8,128)(2,1)S(1)} %copy-done, f32[2,128]{1,0:T(2,128)S(1)} %reshape.19.flags_ref), custom_call_target="tpu_custom_call" | custom-call | tf_op jit(solution)/shard_map/beams/pallas_call | solution.py:247
  77.5 34.6 %all_to_all.10 = bf16[512,4,128]{2,1,0:T(4,128)(2,1)S(1)} all-to-all(bf16[512,4,128]{2,1,0:T(4,128)(2,1)S(1)} %bitcast.10), channel_id=1, replica_groups=mesh['gx'=32,'gy'=16] {'gx','gy'}, dimensions={0} | all-to-all | bytes 1048576 | tf_op jit(solution)/shard_map/all_to_all | solution.py:335
  112.1 2.2 %finish.1 = (bf16[2,8,16384]{2,1,0:T(8,128)(2,1)}, f32[2,2,16384]{2,1,0:T(2,128)}) custom-call(bf16[2048,128]{1,0:T(8,128)(2,1)S(1)} %bitcast.9), custom_call_target="tpu_custom_call" | custom-call | tf_op jit(solution)/shard_map/finish/pallas_call | solution.py:313
  (2 shorter events, 0.0 us)
Async XLA Ops:
  3.2 14.6 %copy-start.3 = (s32[8,32]{1,0:T(8,128)S(1)}, s32[8,32]{1,0:T(8,128)}, u32[]{:S(2)}) copy-start(s32[8,32]{1,0:T(8,128)} %param.8) | copy-start | bytes 3076
  3.3 14.8 %copy-start.1 = (s32[2048,2]{0,1:T(2,128)S(1)}, s32[2048,2]{0,1:T(2,128)}, u32[]{:S(2)}) copy-start(s32[2048,2]{0,1:T(2,128)} %param.7) | copy-start | bytes 49156
  3.3 14.8 %copy-start.2 = (s32[1024,2]{0,1:T(2,128)S(1)}, s32[1024,2]{0,1:T(2,128)}, u32[]{:S(2)}) copy-start(s32[1024,2]{0,1:T(2,128)} %param.6) | copy-start | bytes 24580
  3.3 65.5 %all-to-all-start = ((bf16[64,64,256]{2,1,0:T(8,128)(2,1)}), bf16[64,64,256]{2,1,0:T(8,128)(2,1)S(1)}, u32[]{:S(2)}, u32[]{:S(2)}) async-start(bf16[64,64,256]{2,1,0:T(8,128)(2,1)} %regroup.1), calls=%async_computation | async-start | bytes 4194304 | tf_op jit(solution)/shard_map/all_to_all | solution.py:329
  18.1 50.7 %copy-start = (bf16[512,256]{1,0:T(8,128)(2,1)S(1)}, bf16[512,256]{1,0:T(8,128)(2,1)}, u32[]{:S(2)}) copy-start(bf16[512,256]{1,0:T(8,128)(2,1)} %constant.2.clone.table_ref) | copy-start | bytes 786436

commit v7 on v6

--- a/solution.py
+++ b/solution.py
@@ -167,8 +167,9 @@
 
     kept = head_ref.shape[1]
     for part in range(2):
-        rest = pl.ds(kept, ROWS - kept)
-        pltpu.make_async_copy(w_hbm.at[0, 0, part, rest], w_buf.at[0, part, rest], sem.at[0]).start()
+        for row in range(kept, ROWS, 32):
+            at = (0, part, pl.ds(row, 32))
+            pltpu.make_async_copy(w_hbm.at[0].at[at], w_buf.at[at], sem.at[0]).start()
         first = w_buf.at[0, part, pl.ds(0, kept)]
         pltpu.make_async_copy(head_ref.at[part], first, sem.at[0]).start()
     for i in range(1, slots):

time: 115 us -> 115 us (level)
  no operation moved by 1% of the time
where the time goes in v7:
time: 115 us; the launch traced here: 114 us
  Pallas kernels  38.3 us (33%)
  blocking collectives  34.6 us (30%)
  waiting for transfers between devices  26 us (23%)
  starting transfers between devices  14.6 us (13%)
    all_to_all x1, blocking collectives, per_device(): lax.all_to_all(power, ('gx', 'gy'), split_axis=0, concat_axis=0, tiled=True)  34.6 us
    all_to_all x1, waiting for transfers between devices, per_device(): piece = lax.all_to_all(sent, 'gx', split_axis=0, concat_axis=0, tiled=True)  26 us
    pallas_call x1, Pallas kernels, weights(): pl.pallas_call(functools.partial(weights_kernel, local_chans), grid=(loca...  24.7 us
    all_to_all x1, starting transfers between devices, per_device(): piece = lax.all_to_all(sent, 'gx', split_axis=0, concat_axis=0, tiled=True)  14.6 us
    pallas_call x1, Pallas kernels, form_beams(): pl.pallas_call(beams_kernel, in_specs=[pl.BlockSpec(memory_space=pltpu.HB...  8.8 us
    pallas_call x1, Pallas kernels, regroup(): pl.pallas_call(regroup_kernel, in_specs=[pl.BlockSpec(memory_space=pltpu....  2.61 us
  transfers between devices with their start and end apart: 1, of which 1 were waited for; matrix products, arithmetic and copies ran while one was open for 0% of the time, Pallas kernels for 22%

profile of v7, /device:TPU:1, one launch (start us, length us, event | category | flops | bytes accessed | tf_op | source)
XLA Modules:
  0.0 114.3 jit_solution(13268593418335235074)
XLA Ops:
  0.6 2.6 %regroup.1 = bf16[64,64,256]{2,1,0:T(8,128)(2,1)} custom-call(bf16[2,64,64,128]{3,2,1,0:T(8,128)(2,1)} %v_ref.1), custom_call_target="tpu_custom_call" | custom-call | tf_op jit(solution)/shard_map/regroup/pallas_call | solution.py:65
  3.2 0.0 copy-start.3
  3.3 0.0 copy-start.1
  3.3 0.0 copy-start.2
  3.3 14.6 %all-to-all-start = ((bf16[64,64,256]{2,1,0:T(8,128)(2,1)}), bf16[64,64,256]{2,1,0:T(8,128)(2,1)S(1)}, u32[]{:S(2)}, u32[]{:S(2)}) async-start(bf16[64,64,256]{2,1,0:T(8,128)(2,1)} %regroup.1), calls=%async_computation | async-start | bytes 4194304 | tf_op jit(solution)/shard_map/all_to_all | solution.py:330
  17.9 0.0 copy-done.3
  17.9 0.1 convert_element_type.10
  18.0 0.1 reshape.19.flags_ref
  18.1 0.0 copy-done.1
  18.1 0.0 copy-done.2
  18.1 0.0 copy-start
  18.1 24.7 %weights.1 = (bf16[2,4,2,256,2048]{4,3,2,1,0:T(8,128)(2,1)}, bf16[2,128,2048]{2,1,0:T(8,128)(2,1)S(1)}) custom-call(s32[2,1024]{1,0:T(2,128)S(1)} %bitcast.12, s32[2,2048]{1,0:T(2,128)S(1)} %bitcast.11), custom_call_target="tpu_custom_call" | custom-call | flops 2516582400 | bytes 16777216 | tf_op jit(solution)/shard_map/weights/pallas_call | solution.py:127
  42.7 26.0 %all-to-all-done = bf16[64,64,256]{2,1,0:T(8,128)(2,1)S(1)} async-done(((bf16[64,64,256]{2,1,0:T(8,128)(2,1)}), bf16[64,64,256]{2,1,0:T(8,128)(2,1)S(1)}, u32[]{:S(2)}, u32[]{:S(2)}) %all-to-all-start) | async-done | bytes 2097184 | tf_op jit(solution)/shard_map/all_to_all | solution.py:330
  68.8 0.0 copy-done
  68.8 8.8 %beams.1 = bf16[2048,128]{1,0:T(8,128)(2,1)S(1)} custom-call(bf16[2,4,2,256,2048]{4,3,2,1,0:T(8,128)(2,1)} %get-tuple-element.4.w_hbm, bf16[2,128,2048]{2,1,0:T(8,128)(2,1)S(1)} %get-tuple-element.5.head_ref, bf16[32,2,64,256]{3,2,1,0:T(8,128)(2,1)S(1)} %bitcast.8, bf16[512,256]{1,0:T(8,128)(2,1)S(1)} %copy-done, f32[2,128]{1,0:T(2,128)S(1)} %reshape.19.flags_ref), custom_call_target="tpu_custom_call" | custom-call | tf_op jit(solution)/shard_map/beams/pallas_call | solution.py:248
  77.6 34.6 %all_to_all.10 = bf16[512,4,128]{2,1,0:T(4,128)(2,1)S(1)} all-to-all(bf16[512,4,128]{2,1,0:T(4,128)(2,1)S(1)} %bitcast.10), channel_id=1, replica_groups=mesh['gx'=32,'gy'=16] {'gx','gy'}, dimensions={0} | all-to-all | bytes 1048576 | tf_op jit(solution)/shard_map/all_to_all | solution.py:336
  112.1 2.2 %finish.1 = (bf16[2,8,16384]{2,1,0:T(8,128)(2,1)}, f32[2,2,16384]{2,1,0:T(2,128)}) custom-call(bf16[2048,128]{1,0:T(8,128)(2,1)S(1)} %bitcast.9), custom_call_target="tpu_custom_call" | custom-call | tf_op jit(solution)/shard_map/finish/pallas_call | solution.py:314
  (2 shorter events, 0.0 us)
Async XLA Ops:
  3.2 14.6 %copy-start.3 = (s32[8,32]{1,0:T(8,128)S(1)}, s32[8,32]{1,0:T(8,128)}, u32[]{:S(2)}) copy-start(s32[8,32]{1,0:T(8,128)} %param.8) | copy-start | bytes 3076
  3.3 14.8 %copy-start.1 = (s32[2048,2]{0,1:T(2,128)S(1)}, s32[2048,2]{0,1:T(2,128)}, u32[]{:S(2)}) copy-start(s32[2048,2]{0,1:T(2,128)} %param.7) | copy-start | bytes 49156
  3.3 14.8 %copy-start.2 = (s32[1024,2]{0,1:T(2,128)S(1)}, s32[1024,2]{0,1:T(2,128)}, u32[]{:S(2)}) copy-start(s32[1024,2]{0,1:T(2,128)} %param.6) | copy-start | bytes 24580
  3.3 65.5 %all-to-all-start = ((bf16[64,64,256]{2,1,0:T(8,128)(2,1)}), bf16[64,64,256]{2,1,0:T(8,128)(2,1)S(1)}, u32[]{:S(2)}, u32[]{:S(2)}) async-start(bf16[64,64,256]{2,1,0:T(8,128)(2,1)} %regroup.1), calls=%async_computation | async-start | bytes 4194304 | tf_op jit(solution)/shard_map/all_to_all | solution.py:330
  18.1 50.7 %copy-start = (bf16[512,256]{1,0:T(8,128)(2,1)S(1)}, bf16[512,256]{1,0:T(8,128)(2,1)}, u32[]{:S(2)}) copy-start(bf16[512,256]{1,0:T(8,128)(2,1)} %constant.2.clone.table_ref) | copy-start | bytes 786436

commit v8 on v6

--- a/solution.py
+++ b/solution.py
@@ -242,7 +242,7 @@
 
 
 def form_beams(w, head, v, flags):
-    slots = 4
+    slots = 6
     vmem = pl.BlockSpec(memory_space=pltpu.VMEM)
     return pl.pallas_call(
         beams_kernel,

time: 115 us -> 115 us (level)
  no operation moved by 1% of the time
where the time goes in v8:
time: 115 us; the launch traced here: 114 us
  Pallas kernels  38.2 us (33%)
  blocking collectives  34.6 us (30%)
  waiting for transfers between devices  26 us (23%)
  starting transfers between devices  14.6 us (13%)
    all_to_all x1, blocking collectives, per_device(): lax.all_to_all(power, ('gx', 'gy'), split_axis=0, concat_axis=0, tiled=True)  34.6 us
    all_to_all x1, waiting for transfers between devices, per_device(): piece = lax.all_to_all(sent, 'gx', split_axis=0, concat_axis=0, tiled=True)  26 us
    pallas_call x1, Pallas kernels, weights(): pl.pallas_call(functools.partial(weights_kernel, local_chans), grid=(loca...  24.7 us
    all_to_all x1, starting transfers between devices, per_device(): piece = lax.all_to_all(sent, 'gx', split_axis=0, concat_axis=0, tiled=True)  14.6 us
    pallas_call x1, Pallas kernels, form_beams(): pl.pallas_call(beams_kernel, in_specs=[pl.BlockSpec(memory_space=pltpu.HB...  8.77 us
    pallas_call x1, Pallas kernels, regroup(): pl.pallas_call(regroup_kernel, in_specs=[pl.BlockSpec(memory_space=pltpu....  2.61 us
  transfers between devices with their start and end apart: 1, of which 1 were waited for; matrix products, arithmetic and copies ran while one was open for 0% of the time, Pallas kernels for 22%

profile of v8, /device:TPU:1, one launch (start us, length us, event | category | flops | bytes accessed | tf_op | source)
XLA Modules:
  0.0 114.3 jit_solution(3179472728514621837)
XLA Ops:
  0.6 2.6 %regroup.1 = bf16[64,64,256]{2,1,0:T(8,128)(2,1)} custom-call(bf16[2,64,64,128]{3,2,1,0:T(8,128)(2,1)} %v_ref.1), custom_call_target="tpu_custom_call" | custom-call | tf_op jit(solution)/shard_map/regroup/pallas_call | solution.py:65
  3.2 0.0 copy-start.3
  3.3 0.0 copy-start.1
  3.3 0.0 copy-start.2
  3.3 14.6 %all-to-all-start = ((bf16[64,64,256]{2,1,0:T(8,128)(2,1)}), bf16[64,64,256]{2,1,0:T(8,128)(2,1)S(1)}, u32[]{:S(2)}, u32[]{:S(2)}) async-start(bf16[64,64,256]{2,1,0:T(8,128)(2,1)} %regroup.1), calls=%async_computation | async-start | bytes 4194304 | tf_op jit(solution)/shard_map/all_to_all | solution.py:329
  17.9 0.0 copy-done.3
  17.9 0.1 convert_element_type.10
  18.0 0.1 reshape.19.flags_ref
  18.1 0.0 copy-done.1
  18.1 0.0 copy-done.2
  18.1 0.0 copy-start
  18.1 24.7 %weights.1 = (bf16[2,4,2,256,2048]{4,3,2,1,0:T(8,128)(2,1)}, bf16[2,128,2048]{2,1,0:T(8,128)(2,1)S(1)}) custom-call(s32[2,1024]{1,0:T(2,128)S(1)} %bitcast.12, s32[2,2048]{1,0:T(2,128)S(1)} %bitcast.11), custom_call_target="tpu_custom_call" | custom-call | flops 2516582400 | bytes 16777216 | tf_op jit(solution)/shard_map/weights/pallas_call | solution.py:127
  42.7 26.0 %all-to-all-done = bf16[64,64,256]{2,1,0:T(8,128)(2,1)S(1)} async-done(((bf16[64,64,256]{2,1,0:T(8,128)(2,1)}), bf16[64,64,256]{2,1,0:T(8,128)(2,1)S(1)}, u32[]{:S(2)}, u32[]{:S(2)}) %all-to-all-start) | async-done | bytes 2097184 | tf_op jit(solution)/shard_map/all_to_all | solution.py:329
  68.8 0.0 copy-done
  68.8 8.8 %beams.1 = bf16[2048,128]{1,0:T(8,128)(2,1)S(1)} custom-call(bf16[2,4,2,256,2048]{4,3,2,1,0:T(8,128)(2,1)} %get-tuple-element.4.w_hbm, bf16[2,128,2048]{2,1,0:T(8,128)(2,1)S(1)} %get-tuple-element.5.head_ref, bf16[32,2,64,256]{3,2,1,0:T(8,128)(2,1)S(1)} %bitcast.8, bf16[512,256]{1,0:T(8,128)(2,1)S(1)} %copy-done, f32[2,128]{1,0:T(2,128)S(1)} %reshape.19.flags_ref), custom_call_target="tpu_custom_call" | custom-call | tf_op jit(solution)/shard_map/beams/pallas_call | solution.py:247
  77.6 34.6 %all_to_all.10 = bf16[512,4,128]{2,1,0:T(4,128)(2,1)S(1)} all-to-all(bf16[512,4,128]{2,1,0:T(4,128)(2,1)S(1)} %bitcast.10), channel_id=1, replica_groups=mesh['gx'=32,'gy'=16] {'gx','gy'}, dimensions={0} | all-to-all | bytes 1048576 | tf_op jit(solution)/shard_map/all_to_all | solution.py:335
  112.1 2.2 %finish.1 = (bf16[2,8,16384]{2,1,0:T(8,128)(2,1)}, f32[2,2,16384]{2,1,0:T(2,128)}) custom-call(bf16[2048,128]{1,0:T(8,128)(2,1)S(1)} %bitcast.9), custom_call_target="tpu_custom_call" | custom-call | tf_op jit(solution)/shard_map/finish/pallas_call | solution.py:313
  (2 shorter events, 0.0 us)
Async XLA Ops:
  3.2 14.6 %copy-start.3 = (s32[8,32]{1,0:T(8,128)S(1)}, s32[8,32]{1,0:T(8,128)}, u32[]{:S(2)}) copy-start(s32[8,32]{1,0:T(8,128)} %param.8) | copy-start | bytes 3076
  3.3 14.8 %copy-start.1 = (s32[2048,2]{0,1:T(2,128)S(1)}, s32[2048,2]{0,1:T(2,128)}, u32[]{:S(2)}) copy-start(s32[2048,2]{0,1:T(2,128)} %param.7) | copy-start | bytes 49156
  3.3 14.8 %copy-start.2 = (s32[1024,2]{0,1:T(2,128)S(1)}, s32[1024,2]{0,1:T(2,128)}, u32[]{:S(2)}) copy-start(s32[1024,2]{0,1:T(2,128)} %param.6) | copy-start | bytes 24580
  3.3 65.5 %all-to-all-start = ((bf16[64,64,256]{2,1,0:T(8,128)(2,1)}), bf16[64,64,256]{2,1,0:T(8,128)(2,1)S(1)}, u32[]{:S(2)}, u32[]{:S(2)}) async-start(bf16[64,64,256]{2,1,0:T(8,128)(2,1)} %regroup.1), calls=%async_computation | async-start | bytes 4194304 | tf_op jit(solution)/shard_map/all_to_all | solution.py:329
  18.1 50.7 %copy-start = (bf16[512,256]{1,0:T(8,128)(2,1)S(1)}, bf16[512,256]{1,0:T(8,128)(2,1)}, u32[]{:S(2)}) copy-start(bf16[512,256]{1,0:T(8,128)(2,1)} %constant.2.clone.table_ref) | copy-start | bytes 786436
